TPU v7x, 32 devices: a whole 2x2x4 slice. The times are simulated.
32 devices in a mesh: tile: 8 (over z, core), dp: 4 (over y, x).
Axes of the slice: x: 2, y: 2, z: 4, core: 2. Of those that a mesh axis runs over, the one named last changes fastest.
Arguments:
- clip_frames: bfloat16 [4, 8, 32, 8, 128], P('dp', None, 'tile'), may hold values from -6 to 6
- segments: int32 [4, 8], P('dp'), may hold values from 0 to 2, never falling along the last dimension, each value on 1 to 4 neighbouring positions
- weight_first: bfloat16 [3456, 128], replicated, may hold values from -0.109375 to 0.109375
- weight_second: bfloat16 [3456, 128], replicated, may hold values from -0.109375 to 0.109375
- cotangent: bfloat16 [4, 8, 16, 4, 128], P('dp', None, 'tile'), may hold values from -6 to 6
Outputs:
- pooled: float32 [4, 8, 16, 4, 128], P('dp', None, 'tile')
- input_grad: float32 [4, 8, 32, 8, 128], P('dp', None, 'tile')
- grad_first: float32 [3456, 128], P('tile')
- grad_second: float32 [3456, 128], P('tile')
Inputs may be any that keep to these rules, and one draw needn't show every extreme that they name: `segments`: clip numbers never fall along the frames of a sequence; each clip is one to 4 frames long and one clip has exactly 4.
All inputs are finite; a program needn't handle non-finite values.
Results may differ from a plain program's by a relative error of at most 0.0029.
Values may be sent and summed in bfloat16 or wider, within the bound.
A program may use at most 64 MiB of HBM per device.

v0:
```python
import functools
import math

import jax
import jax.numpy as jnp
from jax import lax
from jax.experimental import pallas as pl
from jax.experimental.pallas import tpu as pltpu
from jax.sharding import PartitionSpec as P

MESH = pl.DeviceIdType.MESH
F32 = jnp.float32
BF16 = jnp.bfloat16


def up16(n):
    return -(-n // 16) * 16


def shifted_cols(cells, step):
    if step == 0:
        return cells
    cols = cells.shape[2]
    col = lax.broadcasted_iota(jnp.int32, cells.shape, 2)
    moved = pltpu.roll(cells, (-step) % cols, 2)
    keep = (col < cols - 1) if step == 1 else (col > 0)
    return jnp.where(keep, moved, 0.0)


def fill_columns(dst, cells, same, reverse):
    rows, frames, cols, ch = cells.shape
    for ci in range(3):
        moved = shifted_cols(cells, (1 - ci) if reverse else (ci - 1))
        for t in range(3):
            zero = jnp.zeros((rows, cols, ch), F32)
            parts = []
            for f in range(frames):
                src = f + t if reverse else f - t
                if src < 0 or src >= frames:
                    parts.append(zero)
                elif t == 0:
                    parts.append(moved[:, src])
                else:
                    parts.append(moved[:, src] * same[t][max(f, src)])
            block = jnp.stack(parts, axis=1).reshape(rows * frames * cols, ch)
            at = (t * 3 + ci) * ch
            dst[:, at : at + ch] = block.astype(BF16)


def conv_dots(cols_ref, w_ref, start, rows, slab, reverse):
    acc = None
    span = w_ref.shape[1] * 3
    for t in range(3):
        for a in range(3):
            at = (start + (2 - a if reverse else a)) * slab
            term = jnp.dot(
                cols_ref[at : at + rows * slab, t * span : (t + 1) * span],
                w_ref[(t * 3 + a) * span : (t * 3 + a + 1) * span, :],
                preferred_element_type=F32,
            )
            acc = term if acc is None else acc + term
    return acc


def kernel(
    cfg,
    seg, x_hbm, w1_hbm, w2_hbm, g_in,
    pooled, in_grad, out1, out2,
    x_in, w1, w2, in_sem, x_halo, g_halo, cols_x, cols_h, cols_g, cols_a, w1t, w2t, pool_tmp,
    flat1, flat2, send_a, recv_a, sum_a, send_b, recv_b, sum_b, send_c, recv_c, fin,
    h_send, h_recv, a_send, a_recv, b_send, b_recv, c_send, c_recv, d_send, d_recv,
):
    n_tile, n_dp, share, chunk, scale = cfg
    n_z = n_tile // 2
    rows, frames, cols, ch = x_in.shape
    slab = frames * cols
    tile = lax.axis_index("tile")
    dp = lax.axis_index("dp")
    core = lax.rem(tile, 2)
    z = lax.div(tile, 2)
    flats = (flat1, flat2)
    outs = (out1, out2)

    load_x = [
        pltpu.make_async_copy(x_hbm.at[0, :, r], x_in.at[r], in_sem.at[2 + r]) for r in range(rows)
    ]
    load_w1 = pltpu.make_async_copy(w1_hbm, w1, in_sem.at[0])
    load_w2 = pltpu.make_async_copy(w2_hbm, w2, in_sem.at[1])
    for copy in load_x:
        copy.start()
    load_w1.start()
    load_w2.start()

    barrier = pltpu.get_barrier_semaphore()

    def greet(peer):
        pl.semaphore_signal(barrier, inc=1, device_id=peer, device_id_type=MESH)

    @pl.when(tile > 0)
    def _():
        greet({"tile": tile - 1})

    @pl.when(tile < n_tile - 1)
    def _():
        greet({"tile": tile + 1})

    for i in range(1, n_dp):
        greet({"dp": lax.rem(dp + i, n_dp)})
    for j in range(1, n_z):
        greet({"tile": 2 * lax.rem(z + j, n_z) + core})

    span = 3 * ch

    def flip(src, dst):
        for tap in range(27):
            dst[tap * ch : (tap + 1) * ch, :] = src[tap * ch : (tap + 1) * ch, :].T

    for g in range(2):
        if sum_a.shape[2] > share:
            sum_a[g, :, share:, :] = jnp.zeros((n_z, sum_a.shape[2] - share, ch), F32)
        if send_a.shape[2] > share:
            send_a[g, :, share:, :] = jnp.zeros((n_z, send_a.shape[2] - share, ch), BF16)

    @pl.when(tile == 0)
    def _():
        x_halo[0] = jnp.zeros(x_halo.shape[1:], BF16)
        g_halo[0] = jnp.zeros(g_halo.shape[1:], BF16)

    @pl.when(tile == n_tile - 1)
    def _():
        x_halo[1] = jnp.zeros(x_halo.shape[1:], BF16)
        g_halo[1] = jnp.zeros(g_halo.shape[1:], BF16)

    for copy in load_x:
        copy.wait()
    beside = jnp.where(tile > 0, 1, 0) + jnp.where(tile < n_tile - 1, 1, 0)
    pl.semaphore_wait(barrier, n_dp - 1 + n_z - 1 + beside)

    g_rows = g_in.shape[0]

    def halo(side):
        peer = {"tile": tile - 1 if side == 0 else tile + 1}
        return (
            pltpu.make_async_remote_copy(
                src_ref=x_in.at[0:2] if side == 0 else x_in.at[rows - 2 : rows],
                dst_ref=x_halo.at[1 - side],
                send_sem=h_send.at[side], recv_sem=h_recv.at[1 - side],
                device_id=peer, device_id_type=MESH,
            ),
            pltpu.make_async_remote_copy(
                src_ref=g_in.at[0:1] if side == 0 else g_in.at[g_rows - 1 : g_rows],
                dst_ref=g_halo.at[1 - side],
                send_sem=h_send.at[2 + side], recv_sem=h_recv.at[2 + 1 - side],
                device_id=peer, device_id_type=MESH,
            ),
        )

    @pl.when(tile > 0)
    def _():
        for copy in halo(0):
            copy.start()

    @pl.when(tile < n_tile - 1)
    def _():
        for copy in halo(1):
            copy.start()

    load_w1.wait()
    load_w2.wait()
    flip(w2, w2t)
    flip(w1, w1t)
    same = [None]
    for t in range(1, 3):
        same.append(
            [None] * t
            + [jnp.where(seg[0, f] == seg[0, f - t], 1.0, 0.0).astype(F32) for f in range(t, frames)]
        )

    @pl.when(tile > 0)
    def _():
        for copy in halo(0):
            copy.wait_send()
        for copy in halo(1):
            copy.wait_recv()

    @pl.when(tile < n_tile - 1)
    def _():
        for copy in halo(1):
            copy.wait_send()
        for copy in halo(0):
            copy.wait_recv()

    def four(v):
        return v.reshape(v.shape[0], frames, cols, ch)

    mine = x_in[...].astype(F32)
    x_all = jnp.concatenate([x_halo[0].astype(F32), mine, x_halo[1].astype(F32)], axis=0)
    fill_columns(cols_x, x_all, same, False)
    g_all = jnp.concatenate([g_halo[0], g_in[...], g_halo[1]], axis=0).astype(F32)
    g_all = jnp.stack([g_all, g_all], axis=1).reshape(2 * g_all.shape[0], slab, ch)

    wide = rows + 2
    first = conv_dots(cols_x, w1, 0, wide, slab, False)
    sigma = 1.0 / (1.0 + jnp.exp(-first))
    top = jnp.where(tile > 0, 1.0, 0.0).astype(F32)
    low = jnp.where(tile < n_tile - 1, 1.0, 0.0).astype(F32)

    def edges(v):
        v = v.reshape(wide, slab, ch)
        return jnp.concatenate([v[:1] * top, v[1:-1], v[-1:] * low], axis=0)

    def kernel_grad(flat, cols_ref, start, g):
        for t in range(3):
            for a in range(3):
                at = (start + a) * slab
                flat[(t * 3 + a) * span : (t * 3 + a + 1) * span, :] = lax.dot_general(
                    cols_ref[at : at + rows * slab, t * span : (t + 1) * span],
                    g,
                    (((0,), (0,)), ((), ())),
                    preferred_element_type=F32,
                )

    def copies_a(g):
        return [
            pltpu.make_async_remote_copy(
                src_ref=send_a.at[g, k],
                dst_ref=recv_a.at[g, k],
                send_sem=a_send.at[g, k], recv_sem=a_recv.at[g, k],
                device_id={"tile": tile + 1 - 2 * core}, device_id_type=MESH,
            )
            for k in range(n_z)
        ]

    def copies_b(g):
        return [
            pltpu.make_async_remote_copy(
                src_ref=send_b.at[g, i - 1], dst_ref=recv_b.at[g, i - 1],
                send_sem=b_send.at[g, i - 1], recv_sem=b_recv.at[g, i - 1],
                device_id={"dp": lax.rem(dp + i, n_dp)}, device_id_type=MESH,
            )
            for i in range(1, n_dp)
        ]

    def copies_c(g):
        return [
            pltpu.make_async_remote_copy(
                src_ref=send_c.at[g, j - 1], dst_ref=recv_c.at[g, j - 1],
                send_sem=c_send.at[g, j - 1], recv_sem=c_recv.at[g, j - 1],
                device_id={"tile": 2 * lax.rem(z + j, n_z) + core}, device_id_type=MESH,
            )
            for j in range(1, n_z)
        ]

    def part(q):
        return pl.ds(pl.multiple_of(q * chunk, 16), chunk)

    def copies_d(g):
        return [
            pltpu.make_async_remote_copy(
                src_ref=fin.at[g, part(dp)], dst_ref=fin.at[g, part(dp)],
                send_sem=d_send.at[g, i - 1], recv_sem=d_recv.at[g, i - 1],
                device_id={"dp": lax.rem(dp + i, n_dp)}, device_id_type=MESH,
            )
            for i in range(1, n_dp)
        ]

    def start(copies):
        for copy in copies:
            copy.start()

    def wait(copies):
        for copy in copies:
            copy.wait()

    def step_b(g):
        wait(copies_a(g))
        for k in range(n_z):
            own = flats[g][pl.ds(pl.multiple_of((2 * k + core) * share, 8), share), :]
            sum_a[g, k, 0:share, :] = own + recv_a[g, k, 0:share].astype(F32)
        for i in range(1, n_dp):
            send_b[g, i - 1] = sum_a[g, :, part(lax.rem(dp + i, n_dp)), :].astype(BF16)
        start(copies_b(g))

    def step_c(g):
        wait(copies_b(g))
        total = sum_a[g, :, part(dp), :]
        for i in range(1, n_dp):
            total = total + recv_b[g, i - 1].astype(F32)
        sum_b[g] = total
        for j in range(1, n_z):
            send_c[g, j - 1] = sum_b[g, lax.rem(z + j, n_z)].astype(BF16)
        start(copies_c(g))

    def step_d(g):
        wait(copies_c(g))
        total = sum_b[g, z]
        for j in range(1, n_z):
            total = total + recv_c[g, j - 1].astype(F32)
        fin[g, part(dp), :] = total * scale
        start(copies_d(g))

    def step_a(g):
        for k, copy in enumerate(copies_a(g)):
            at = pl.ds(pl.multiple_of((2 * k + 1 - core) * share, 8), share)
            send_a[g, k, 0:share, :] = flats[g][at, :].astype(BF16)
            copy.start()

    hidden = edges(first * sigma)
    fill_columns(cols_h, four(hidden), same, False)
    g_own = g_all[2 : 2 + rows].reshape(rows * slab, ch)
    kernel_grad(flat2, cols_h, 0, g_own.astype(BF16))
    step_a(1)
    fill_columns(cols_g, four(g_all), same, True)
    hidden_grad = conv_dots(cols_g, w2t, 0, wide, slab, True)
    act = edges(hidden_grad * sigma * (1.0 + first * (1.0 - sigma)))
    act_own = act[1 : 1 + rows].reshape(rows * slab, ch).astype(BF16)

    step_b(1)
    kernel_grad(flat1, cols_x, 1, act_own)
    step_a(0)
    fill_columns(cols_a, four(act), same, True)
    step_b(0)
    second = conv_dots(cols_h, w2, 0, rows, slab, False)
    summed = mine.reshape(rows, slab, ch) + second.reshape(rows, slab, ch)
    pairs = rows // 2
    for i in range(pairs):
        pool_tmp[i * slab : (i + 1) * slab, :] = summed[2 * i] + summed[2 * i + 1]
    for i in range(pairs):
        for f in range(frames):
            at = i * slab + f * cols
            pooled[0, f, i] = 0.25 * (
                pool_tmp[pl.ds(at, cols // 2, stride=2), :]
                + pool_tmp[pl.ds(at + 1, cols // 2, stride=2), :]
            )
    step_c(1)
    back = conv_dots(cols_a, w1t, 0, rows, slab, True)
    total = (g_own + back).reshape(rows, frames, cols, ch)
    for r in range(rows):
        in_grad[0, :, r] = total[r]
    step_c(0)
    step_d(1)
    step_d(0)
    for g in (1, 0):
        wait(copies_d(g))
        outs[g][...] = fin[g, 0:share, :]


def local(n_tile, n_dp, clip_frames, segments, weight_first, weight_second, cotangent):
    _, frames, rows, cols, ch = clip_frames.shape
    slab = frames * cols
    taps = weight_first.shape[0]
    share = taps // n_tile
    chunk = up16(-(-share // n_dp))
    n_z = n_tile // 2
    g = jnp.repeat(cotangent[0].transpose(1, 0, 2, 3), 2, axis=2) * jnp.bfloat16(0.25)
    g = g.reshape(rows // 2, slab, ch)
    scale = 1.0 / math.sqrt(n_dp * n_tile * rows * slab)
    vmem = pl.BlockSpec(memory_space=pltpu.VMEM)
    cells = rows * slab
    sem = pltpu.SemaphoreType.DMA
    anywhere = pl.BlockSpec(memory_space=pltpu.HBM)
    shapes = (
        jax.ShapeDtypeStruct((1, frames, rows // 2, cols // 2, ch), F32),
        jax.ShapeDtypeStruct((1, frames, rows, cols, ch), F32),
        jax.ShapeDtypeStruct((share, ch), F32),
        jax.ShapeDtypeStruct((share, ch), F32),
    )
    results = pl.pallas_call(
        functools.partial(kernel, (n_tile, n_dp, share, chunk, scale)),
        out_shape=shapes,
        in_specs=[pl.BlockSpec(memory_space=pltpu.SMEM)] + [anywhere] * 3 + [vmem],
        out_specs=(vmem,) * 4,
        scratch_shapes=[
            pltpu.VMEM((rows, frames, cols, ch), BF16),
            pltpu.VMEM((taps, ch), BF16),
            pltpu.VMEM((taps, ch), BF16),
            sem((2 + rows,)),
            pltpu.VMEM((2, 2, frames, cols, ch), BF16),
            pltpu.VMEM((2, 1, slab, ch), BF16),
            pltpu.VMEM(((rows + 4) * slab, 9 * ch), BF16),
            pltpu.VMEM(((rows + 2) * slab, 9 * ch), BF16),
            pltpu.VMEM(((rows + 4) * slab, 9 * ch), BF16),
            pltpu.VMEM(((rows + 2) * slab, 9 * ch), BF16),
            pltpu.VMEM((taps, ch), BF16),
            pltpu.VMEM((taps, ch), BF16),
            pltpu.VMEM((cells // 2, ch), F32),
            pltpu.VMEM((taps, ch), F32),
            pltpu.VMEM((taps, ch), F32),
            pltpu.VMEM((2, n_z, up16(share), ch), BF16),
            pltpu.VMEM((2, n_z, up16(share), ch), BF16),
            pltpu.VMEM((2, n_z, n_dp * chunk, ch), F32),
            pltpu.VMEM((2, n_dp - 1, n_z, chunk, ch), BF16),
            pltpu.VMEM((2, n_dp - 1, n_z, chunk, ch), BF16),
            pltpu.VMEM((2, n_z, chunk, ch), F32),
            pltpu.VMEM((2, n_z - 1, chunk, ch), BF16),
            pltpu.VMEM((2, n_z - 1, chunk, ch), BF16),
            pltpu.VMEM((2, n_dp * chunk, ch), F32),
            sem((4,)), sem((4,)),
            sem((2, n_z)), sem((2, n_z)),
            sem((2, n_dp - 1)), sem((2, n_dp - 1)),
            sem((2, n_z - 1)), sem((2, n_z - 1)),
            sem((2, n_dp - 1)), sem((2, n_dp - 1)),
        ],
        compiler_params=pltpu.CompilerParams(
            collective_id=0, has_side_effects=True, vmem_limit_bytes=50 * 1024 * 1024
        ),
    )(segments, clip_frames, weight_first, weight_second, g)
    return tuple(results)


def solution(mesh):
    return jax.shard_map(
        functools.partial(local, mesh.shape["tile"], mesh.shape["dp"]),
        mesh=mesh,
        in_specs=(
            P("dp", None, "tile", None, None),
            P("dp", None),
            P(),
            P(),
            P("dp", None, "tile", None, None),
        ),
        out_specs=(
            P("dp", None, "tile", None, None),
            P("dp", None, "tile", None, None),
            P("tile", None),
            P("tile", None),
        ),
        check_vma=False,
    )
```

profile of v0, /device:TPU:0, one launch (start us, length us, event | category | flops | bytes accessed | tf_op | source)
XLA Modules:
  0.0 40.3 jit_solution(8909111648645172535)
XLA Ops:
  0.6 0.0 copy-start.2
  0.6 0.8 %multiply_bitcast_fusion = bf16[2,8,4,128]{3,2,0,1:T(4,128)(2,1)S(1)} fusion(bf16[1,8,2,4,128]{4,3,2,1,0:T(4,128)(2,1)} %param.9), kind=kLoop, calls=%fused_computation | loop fusion | flops 8192 | bytes 32768 | tf_op jit(solution)/shard_map/mul | solution.py:355
  1.4 0.0 copy-start.3
  1.5 0.0 copy-done.2
  1.5 0.6 %copy-done.3 = s32[1,8]{1,0:T(1,128)S(1)} copy-done((s32[1,8]{1,0:T(1,128)S(1)}, s32[1,8]{1,0:T(1,128)}, u32[]{:S(2)}) %copy-start.3) | copy-done | bytes 56
  2.1 0.0 copy-start
  2.1 1.2 %copy-done = bf16[3456,128]{1,0:T(8,128)(2,1)S(1)} copy-done((bf16[3456,128]{1,0:T(8,128)(2,1)S(1)}, bf16[3456,128]{1,0:T(8,128)(2,1)}, u32[]{:S(2)}) %copy-start) | copy-done | bytes 884760
  3.3 0.0 copy-start.1
  3.3 1.2 %copy-done.1 = bf16[3456,128]{1,0:T(8,128)(2,1)S(1)} copy-done((bf16[3456,128]{1,0:T(8,128)(2,1)S(1)}, bf16[3456,128]{1,0:T(8,128)(2,1)}, u32[]{:S(2)}) %copy-start.1) | copy-done | bytes 884760
  4.4 33.2 %shard_map.84 = (f32[1,8,2,4,128]{4,3,2,1,0:T(4,128)S(1)}, f32[1,8,4,8,128]{4,3,2,1,0:T(8,128)S(1)}, f32[432,128]{1,0:T(8,128)S(1)}, f32[432,128]{1,0:T(8,128)S(1)}) custom-call(s32[1,8]{1,0:T(1,128)S(1)} %copy-done.3, bf16[1,8,4,8,128]{4,3,2,1,0:T(8,128)(2,1)S(1)} %copy-done.2, bf16[3456,128]{1,0:T(8,128)(2,1)S(1)} %copy-done, ...), custom_call_target="tpu_custom_call" | custom-call | tf_op jit(solution)/shard_map/pallas_call | solution.py:368
  37.7 0.6 %copy.14 = f32[1,8,2,4,128]{4,3,2,1,0:T(4,128)} copy(f32[1,8,2,4,128]{4,3,2,1,0:T(4,128)S(1)} %get-tuple-element.8) | data formatting | bytes 65536
  38.3 0.7 %copy.15 = f32[1,8,4,8,128]{4,3,2,1,0:T(8,128)} copy(f32[1,8,4,8,128]{4,3,2,1,0:T(8,128)S(1)} %get-tuple-element.9) | data formatting | bytes 262144
  39.0 0.7 %copy.16 = f32[432,128]{1,0:T(8,128)} copy(f32[432,128]{1,0:T(8,128)S(1)} %get-tuple-element.10) | data formatting | bytes 442368
  39.6 0.7 %copy.17 = f32[432,128]{1,0:T(8,128)} copy(f32[432,128]{1,0:T(8,128)S(1)} %get-tuple-element.11) | data formatting | bytes 442368
  (2 shorter events, 0.0 us)
Async XLA Ops:
  0.6 0.8 %copy-start.2 = (bf16[1,8,4,8,128]{4,3,2,1,0:T(8,128)(2,1)S(1)}, bf16[1,8,4,8,128]{4,3,2,1,0:T(8,128)(2,1)}, u32[]{:S(2)}) copy-start(bf16[1,8,4,8,128]{4,3,2,1,0:T(8,128)(2,1)} %x_hbm.1) | copy-start | bytes 196612
  1.4 0.7 %copy-start.3 = (s32[1,8]{1,0:T(1,128)S(1)}, s32[1,8]{1,0:T(1,128)}, u32[]{:S(2)}) copy-start(s32[1,8]{1,0:T(1,128)} %seg.1) | copy-start | bytes 100
  2.1 1.2 %copy-start = (bf16[3456,128]{1,0:T(8,128)(2,1)S(1)}, bf16[3456,128]{1,0:T(8,128)(2,1)}, u32[]{:S(2)}) copy-start(bf16[3456,128]{1,0:T(8,128)(2,1)} %w1_hbm.1) | copy-start | bytes 2654212
  3.3 1.2 %copy-start.1 = (bf16[3456,128]{1,0:T(8,128)(2,1)S(1)}, bf16[3456,128]{1,0:T(8,128)(2,1)}, u32[]{:S(2)}) copy-start(bf16[3456,128]{1,0:T(8,128)(2,1)} %w2_hbm.1) | copy-start | bytes 2654212
where the time goes:
time: 40.6 us; the launch traced here: 40.3 us
  Pallas kernels  33.2 us (82%)
  local copies, waits for them, and re-layouts  5.66 us (14%)
  other arithmetic  0.76 us (2%)
  between operations  0.68 us (2%)
    pallas_call x1, Pallas kernels, local(): pl.pallas_call(functools.partial(kernel, (n_tile, n_dp, share, chunk, sca...  33.2 us
    unnamed x12, local copies, waits for them, and re-layouts  5.63 us

commit v1 on v0

--- a/solution.py
+++ b/solution.py
@@ -64,9 +64,9 @@
 
 def kernel(
     cfg,
-    seg, x_hbm, w1_hbm, w2_hbm, g_in,
-    pooled, in_grad, out1, out2,
-    x_in, w1, w2, in_sem, x_halo, g_halo, cols_x, cols_h, cols_g, cols_a, w1t, w2t, pool_tmp,
+    seg, x_hbm, w1_hbm, w2_hbm, c_hbm,
+    pooled_hbm, in_grad_hbm, out1, out2,
+    pooled, in_grad, out_sem, x_in, w1, w2, c_in, g_tmp, in_sem, x_halo, g_halo, cols_x, cols_h, cols_g, cols_a, w1t, w2t, pool_tmp,
     flat1, flat2, send_a, recv_a, sum_a, send_b, recv_b, sum_b, send_c, recv_c, fin,
     h_send, h_recv, a_send, a_recv, b_send, b_recv, c_send, c_recv, d_send, d_recv,
 ):
@@ -84,9 +84,13 @@
     load_x = [
         pltpu.make_async_copy(x_hbm.at[0, :, r], x_in.at[r], in_sem.at[2 + r]) for r in range(rows)
     ]
+    load_c = [
+        pltpu.make_async_copy(c_hbm.at[0, :, r], c_in.at[r], in_sem.at[2 + rows + r])
+        for r in range(rows // 2)
+    ]
     load_w1 = pltpu.make_async_copy(w1_hbm, w1, in_sem.at[0])
     load_w2 = pltpu.make_async_copy(w2_hbm, w2, in_sem.at[1])
-    for copy in load_x:
+    for copy in load_x + load_c:
         copy.start()
     load_w1.start()
     load_w2.start()
@@ -131,12 +135,12 @@
         x_halo[1] = jnp.zeros(x_halo.shape[1:], BF16)
         g_halo[1] = jnp.zeros(g_halo.shape[1:], BF16)
 
-    for copy in load_x:
+    for copy in load_x + load_c:
         copy.wait()
     beside = jnp.where(tile > 0, 1, 0) + jnp.where(tile < n_tile - 1, 1, 0)
     pl.semaphore_wait(barrier, n_dp - 1 + n_z - 1 + beside)
 
-    g_rows = g_in.shape[0]
+    g_rows = c_in.shape[0]
 
     def halo(side):
         peer = {"tile": tile - 1 if side == 0 else tile + 1}
@@ -148,7 +152,7 @@
                 device_id=peer, device_id_type=MESH,
             ),
             pltpu.make_async_remote_copy(
-                src_ref=g_in.at[0:1] if side == 0 else g_in.at[g_rows - 1 : g_rows],
+                src_ref=c_in.at[0:1] if side == 0 else c_in.at[g_rows - 1 : g_rows],
                 dst_ref=g_halo.at[1 - side],
                 send_sem=h_send.at[2 + side], recv_sem=h_recv.at[2 + 1 - side],
                 device_id=peer, device_id_type=MESH,
@@ -196,7 +200,12 @@
     mine = x_in[...].astype(F32)
     x_all = jnp.concatenate([x_halo[0].astype(F32), mine, x_halo[1].astype(F32)], axis=0)
     fill_columns(cols_x, x_all, same, False)
-    g_all = jnp.concatenate([g_halo[0], g_in[...], g_halo[1]], axis=0).astype(F32)
+    c_all = jnp.concatenate([g_halo[0], c_in[...], g_halo[1]], axis=0).astype(F32) * 0.25
+    half = (g_rows + 2) * slab // 2
+    c_all = c_all.reshape(half, ch)
+    g_tmp[pl.ds(0, half, stride=2), :] = c_all
+    g_tmp[pl.ds(1, half, stride=2), :] = c_all
+    g_all = g_tmp[...].reshape(g_rows + 2, slab, ch)
     g_all = jnp.stack([g_all, g_all], axis=1).reshape(2 * g_all.shape[0], slab, ch)
 
     wide = rows + 2
@@ -328,21 +337,43 @@
     for i in range(pairs):
         for f in range(frames):
             at = i * slab + f * cols
-            pooled[0, f, i] = 0.25 * (
+            pooled[f, i] = 0.25 * (
                 pool_tmp[pl.ds(at, cols // 2, stride=2), :]
                 + pool_tmp[pl.ds(at + 1, cols // 2, stride=2), :]
             )
+    put_pooled = pltpu.make_async_copy(pooled, pooled_hbm.at[0], out_sem.at[2])
+    put_pooled.start()
     step_c(1)
     back = conv_dots(cols_a, w1t, 0, rows, slab, True)
     total = (g_own + back).reshape(rows, frames, cols, ch)
     for r in range(rows):
-        in_grad[0, :, r] = total[r]
+        in_grad[:, r] = total[r]
+    put_grad = pltpu.make_async_copy(in_grad, in_grad_hbm.at[0], out_sem.at[3])
+    put_grad.start()
     step_c(0)
     step_d(1)
     step_d(0)
+    puts = [pltpu.make_async_copy(fin.at[g, 0:share], outs[g], out_sem.at[g]) for g in range(2)]
     for g in (1, 0):
         wait(copies_d(g))
-        outs[g][...] = fin[g, 0:share, :]
+        puts[g].start()
+    put_pooled.wait()
+    put_grad.wait()
+    for g in (1, 0):
+        puts[g].wait()
+
+
+def hand_out(*refs):
+    held, load_sem, store_sem = refs[8:12], refs[12], refs[13]
+    loads = [pltpu.make_async_copy(refs[i], held[i], load_sem.at[i]) for i in range(4)]
+    stores = [pltpu.make_async_copy(held[i], refs[4 + i], store_sem.at[i]) for i in range(4)]
+    for copy in loads:
+        copy.start()
+    for i in (0, 2, 3, 1):
+        loads[i].wait()
+        stores[i].start()
+    for copy in stores:
+        copy.wait()
 
 
 def local(n_tile, n_dp, clip_frames, segments, weight_first, weight_second, cotangent):
@@ -352,8 +383,6 @@
     share = taps // n_tile
     chunk = up16(-(-share // n_dp))
     n_z = n_tile // 2
-    g = jnp.repeat(cotangent[0].transpose(1, 0, 2, 3), 2, axis=2) * jnp.bfloat16(0.25)
-    g = g.reshape(rows // 2, slab, ch)
     scale = 1.0 / math.sqrt(n_dp * n_tile * rows * slab)
     vmem = pl.BlockSpec(memory_space=pltpu.VMEM)
     cells = rows * slab
@@ -368,15 +397,20 @@
     results = pl.pallas_call(
         functools.partial(kernel, (n_tile, n_dp, share, chunk, scale)),
         out_shape=shapes,
-        in_specs=[pl.BlockSpec(memory_space=pltpu.SMEM)] + [anywhere] * 3 + [vmem],
-        out_specs=(vmem,) * 4,
+        in_specs=[pl.BlockSpec(memory_space=pltpu.SMEM)] + [anywhere] * 4,
+        out_specs=(anywhere,) * 4,
         scratch_shapes=[
+            pltpu.VMEM((frames, rows // 2, cols // 2, ch), F32),
+            pltpu.VMEM((frames, rows, cols, ch), F32),
+            sem((4,)),
             pltpu.VMEM((rows, frames, cols, ch), BF16),
             pltpu.VMEM((taps, ch), BF16),
             pltpu.VMEM((taps, ch), BF16),
-            sem((2 + rows,)),
+            pltpu.VMEM((rows // 2, frames, cols // 2, ch), BF16),
+            pltpu.VMEM(((rows // 2 + 2) * slab, ch), F32),
+            sem((2 + rows + rows // 2,)),
             pltpu.VMEM((2, 2, frames, cols, ch), BF16),
-            pltpu.VMEM((2, 1, slab, ch), BF16),
+            pltpu.VMEM((2, 1, frames, cols // 2, ch), BF16),
             pltpu.VMEM(((rows + 4) * slab, 9 * ch), BF16),
             pltpu.VMEM(((rows + 2) * slab, 9 * ch), BF16),
             pltpu.VMEM(((rows + 4) * slab, 9 * ch), BF16),
@@ -402,10 +436,18 @@
             sem((2, n_dp - 1)), sem((2, n_dp - 1)),
         ],
         compiler_params=pltpu.CompilerParams(
-            collective_id=0, has_side_effects=True, vmem_limit_bytes=50 * 1024 * 1024
+            collective_id=0, has_side_effects=True, vmem_limit_bytes=60 * 1024 * 1024
         ),
-    )(segments, clip_frames, weight_first, weight_second, g)
-    return tuple(results)
+    )(segments, clip_frames, weight_first, weight_second, cotangent)
+    return tuple(
+        pl.pallas_call(
+            hand_out,
+            out_shape=shapes,
+            in_specs=[pl.BlockSpec(memory_space=pl.ANY)] * 4,
+            out_specs=(pl.BlockSpec(memory_space=pl.ANY),) * 4,
+            scratch_shapes=[pltpu.VMEM(v.shape, v.dtype) for v in shapes] + [sem((4,))] * 2,
+        )(*results)
+    )
 
 
 def solution(mesh):

time: 40.6 us -> 36.4 us (0.90)
  local copies, waits for them, and re-layouts: 5.66 us -> 0 us
  Pallas kernels: 33.2 us -> 35.6 us
  other arithmetic: 0.76 us -> 0 us
    unnamed x12 -> x0, local copies, waits for them, and re-layouts: 5.63 us -> none
    pallas_call x0 -> x1, Pallas kernels: none -> 1.93 us  [local(): pl.pallas_call(hand_out, out_shape=shapes, in_specs=[pl.BlockSpec(memory_...]
    mul x1 -> x0, other arithmetic: 0.76 us -> none  [local(): jnp.repeat(cotangent[0].transpose(1, 0, 2, 3), 2, axis=2)]
    pallas_call x1, Pallas kernels: 33.2 us -> 33.7 us  [local(): pl.pallas_call(functools.partial(kernel, (n_tile, n_dp, share, chunk, sca...]
where the time goes in v1:
time: 36.4 us; the launch traced here: 36.3 us
  Pallas kernels  35.6 us (98%)
  between operations  0.64 us (2%)
    pallas_call x1, Pallas kernels, local(): pl.pallas_call(functools.partial(kernel, (n_tile, n_dp, share, chunk, sca...  33.7 us
    pallas_call x1, Pallas kernels, local(): pl.pallas_call(hand_out, out_shape=shapes, in_specs=[pl.BlockSpec(memory_...  1.93 us

profile of v1, /device:TPU:0, one launch (start us, length us, event | category | flops | bytes accessed | tf_op | source)
XLA Modules:
  0.0 36.3 jit_solution(14457837575274605418)
XLA Ops:
  0.6 33.7 %shard_map.84 = (f32[1,8,2,4,128]{4,3,2,1,0:T(4,128)}, f32[1,8,4,8,128]{4,3,2,1,0:T(8,128)}, f32[432,128]{1,0:T(8,128)}, f32[432,128]{1,0:T(8,128)}) custom-call(s32[1,8]{1,0:T(1,128)} %seg.1, bf16[1,8,4,8,128]{4,3,2,1,0:T(8,128)(2,1)} %x_hbm.1, bf16[3456,128]{1,0:T(8,128)(2,1)} %w1_hbm.1, bf16[3456,128]{1,0:T(8,128)(2,1)} %w2_hbm.1, ...), custom_call_target="tpu_custom_call" | custom-call | tf_op jit(solution)/shard_map/pallas_call | solution.py:397
  34.3 1.9 %shard_map.85 = (f32[1,8,2,4,128]{4,3,2,1,0:T(4,128)}, f32[1,8,4,8,128]{4,3,2,1,0:T(8,128)}, f32[432,128]{1,0:T(8,128)}, f32[432,128]{1,0:T(8,128)}) custom-call(f32[1,8,2,4,128]{4,3,2,1,0:T(4,128)} %get-tuple-element.8.refs_0_, f32[1,8,4,8,128]{4,3,2,1,0:T(8,128)} %get-tuple-element.9.refs_1_, f32[432,128]{1,0:T(8,128)} %get-tuple-element.10.refs_2_, ...), custom_call_target="tpu_custom_call" | custom-call | tf_op jit(solution)/shard_map/pallas_call | solution.py:443

commit v2 on v1

--- a/solution.py
+++ b/solution.py
@@ -67,10 +67,12 @@
     seg, x_hbm, w1_hbm, w2_hbm, c_hbm,
     pooled_hbm, in_grad_hbm, out1, out2,
     pooled, in_grad, out_sem, x_in, w1, w2, c_in, g_tmp, in_sem, x_halo, g_halo, cols_x, cols_h, cols_g, cols_a, w1t, w2t, pool_tmp,
-    flat1, flat2, send_a, recv_a, sum_a, send_b, recv_b, sum_b, send_c, recv_c, fin,
-    h_send, h_recv, a_send, a_recv, b_send, b_recv, c_send, c_recv, d_send, d_recv,
+    seg_rows, mask_rows, x_out, x_got, hid_out, hid_got, cot_got, act_got, g_got, turned, flat,
+    recv_a, sum_a, send_c, recv_c, every, spread, out_v,
+    h_send, h_recv, x_send, x_recv, s_send, s_recv, k_send, k_recv, g_send, g_recv, t_send, t_recv,
+    a_send, a_recv, c_send, c_recv, d_send, d_recv,
 ):
-    n_tile, n_dp, share, chunk, scale = cfg
+    n_tile, n_dp, share, quarter, part, n_tap, scale = cfg
     n_z = n_tile // 2
     rows, frames, cols, ch = x_in.shape
     slab = frames * cols
@@ -78,8 +80,12 @@
     dp = lax.axis_index("dp")
     core = lax.rem(tile, 2)
     z = lax.div(tile, 2)
-    flats = (flat1, flat2)
+    taps = w1.shape[0] // ch
     outs = (out1, out2)
+    wide = rows + 2
+    cells = rows * slab
+    lanes = wide * slab
+    block = n_tap * part
 
     load_x = [
         pltpu.make_async_copy(x_hbm.at[0, :, r], x_in.at[r], in_sem.at[2 + r]) for r in range(rows)
@@ -119,11 +125,15 @@
         for tap in range(27):
             dst[tap * ch : (tap + 1) * ch, :] = src[tap * ch : (tap + 1) * ch, :].T
 
-    for g in range(2):
-        if sum_a.shape[2] > share:
-            sum_a[g, :, share:, :] = jnp.zeros((n_z, sum_a.shape[2] - share, ch), F32)
-        if send_a.shape[2] > share:
-            send_a[g, :, share:, :] = jnp.zeros((n_z, send_a.shape[2] - share, ch), BF16)
+    if part > quarter:
+        x_out[:, quarter:, :] = jnp.zeros((n_dp, part - quarter, lanes), BF16)
+        hid_out[:, quarter:, :] = jnp.zeros((n_dp, part - quarter, lanes), BF16)
+    lane = lax.broadcasted_iota(jnp.int32, (16, lanes), 1)
+    frame = lax.rem(lax.div(lane, cols), frames)
+    number = jnp.zeros((16, lanes), F32)
+    for f in range(frames):
+        number = jnp.where(frame == f, seg[0, f].astype(F32), number)
+    seg_rows[dp] = number.astype(BF16)
 
     @pl.when(tile == 0)
     def _():
@@ -169,6 +179,30 @@
         for copy in halo(1):
             copy.start()
 
+    def to_dp(src, dst, sends, recvs):
+        return [
+            pltpu.make_async_remote_copy(
+                src_ref=src(lax.rem(dp + i, n_dp)), dst_ref=dst,
+                send_sem=sends.at[i - 1], recv_sem=recvs.at[i - 1],
+                device_id={"dp": lax.rem(dp + i, n_dp)}, device_id_type=MESH,
+            )
+            for i in range(1, n_dp)
+        ]
+
+    def start(copies):
+        for copy in copies:
+            copy.start()
+
+    def wait(copies):
+        for copy in copies:
+            copy.wait()
+
+    copies_cot = to_dp(lambda q: c_in, cot_got.at[dp], k_send, k_recv)
+    copies_seg = to_dp(lambda q: seg_rows.at[dp], seg_rows.at[dp], s_send, s_recv)
+    start(copies_cot)
+    start(copies_seg)
+    cot_got[dp] = c_in[...]
+
     load_w1.wait()
     load_w2.wait()
     flip(w2, w2t)
@@ -199,6 +233,18 @@
 
     mine = x_in[...].astype(F32)
     x_all = jnp.concatenate([x_halo[0].astype(F32), mine, x_halo[1].astype(F32)], axis=0)
+    copies_x = to_dp(lambda q: x_out.at[q], x_got.at[dp], x_send, x_recv)
+    copies_hid = to_dp(lambda q: hid_out.at[q], hid_got.at[dp], t_send, t_recv)
+    copies_act = to_dp(lambda q: act_got.at[dp], act_got.at[dp], g_send, g_recv)
+
+    def deal(v, out, got, copies):
+        v = v.reshape(lanes, ch).T.astype(BF16)
+        for q in range(n_dp):
+            out[q, 0:quarter, :] = v[q * quarter : (q + 1) * quarter]
+        start(copies)
+        got[dp] = out[dp]
+
+    deal(x_all[1 : 1 + wide], x_out, x_got, copies_x)
     fill_columns(cols_x, x_all, same, False)
     c_all = jnp.concatenate([g_halo[0], c_in[...], g_halo[1]], axis=0).astype(F32) * 0.25
     half = (g_rows + 2) * slab // 2
@@ -208,7 +254,6 @@
     g_all = g_tmp[...].reshape(g_rows + 2, slab, ch)
     g_all = jnp.stack([g_all, g_all], axis=1).reshape(2 * g_all.shape[0], slab, ch)
 
-    wide = rows + 2
     first = conv_dots(cols_x, w1, 0, wide, slab, False)
     sigma = 1.0 / (1.0 + jnp.exp(-first))
     top = jnp.where(tile > 0, 1.0, 0.0).astype(F32)
@@ -218,36 +263,20 @@
         v = v.reshape(wide, slab, ch)
         return jnp.concatenate([v[:1] * top, v[1:-1], v[-1:] * low], axis=0)
 
-    def kernel_grad(flat, cols_ref, start, g):
-        for t in range(3):
-            for a in range(3):
-                at = (start + a) * slab
-                flat[(t * 3 + a) * span : (t * 3 + a + 1) * span, :] = lax.dot_general(
-                    cols_ref[at : at + rows * slab, t * span : (t + 1) * span],
-                    g,
-                    (((0,), (0,)), ((), ())),
-                    preferred_element_type=F32,
-                )
+    def tap_0(to):
+        return jnp.minimum(lax.div(share * to, ch), taps - n_tap)
+
+    def window(to):
+        return pl.ds(pl.multiple_of(tap_0(to) * part, 16), block)
 
     def copies_a(g):
         return [
             pltpu.make_async_remote_copy(
-                src_ref=send_a.at[g, k],
-                dst_ref=recv_a.at[g, k],
+                src_ref=flat.at[g, window(2 * k + 1 - core)], dst_ref=recv_a.at[g, k],
                 send_sem=a_send.at[g, k], recv_sem=a_recv.at[g, k],
                 device_id={"tile": tile + 1 - 2 * core}, device_id_type=MESH,
             )
             for k in range(n_z)
-        ]
-
-    def copies_b(g):
-        return [
-            pltpu.make_async_remote_copy(
-                src_ref=send_b.at[g, i - 1], dst_ref=recv_b.at[g, i - 1],
-                send_sem=b_send.at[g, i - 1], recv_sem=b_recv.at[g, i - 1],
-                device_id={"dp": lax.rem(dp + i, n_dp)}, device_id_type=MESH,
-            )
-            for i in range(1, n_dp)
         ]
 
     def copies_c(g):
@@ -260,75 +289,113 @@
             for j in range(1, n_z)
         ]
 
-    def part(q):
-        return pl.ds(pl.multiple_of(q * chunk, 16), chunk)
-
     def copies_d(g):
-        return [
-            pltpu.make_async_remote_copy(
-                src_ref=fin.at[g, part(dp)], dst_ref=fin.at[g, part(dp)],
-                send_sem=d_send.at[g, i - 1], recv_sem=d_recv.at[g, i - 1],
-                device_id={"dp": lax.rem(dp + i, n_dp)}, device_id_type=MESH,
-            )
-            for i in range(1, n_dp)
-        ]
-
-    def start(copies):
-        for copy in copies:
-            copy.start()
-
-    def wait(copies):
-        for copy in copies:
-            copy.wait()
+        return to_dp(lambda q: every.at[g, dp], every.at[g, dp], d_send.at[g], d_recv.at[g])
+
+    def sender(i):
+        return lax.rem(dp + n_dp - i, n_dp)
+
+    def make_masks(d):
+        number = seg_rows[d].astype(F32)[0:8]
+        at = lax.broadcasted_iota(jnp.int32, (8, lanes), 1)
+        when = lax.rem(lax.div(at, cols), frames)
+        col = lax.rem(at, cols)
+        for t in range(3):
+            keep = jnp.ones((8, lanes), F32)
+            if t > 0:
+                keep = jnp.where(number == pltpu.roll(number, t * cols, 1), 1.0, 0.0)
+                keep = jnp.where(when >= t, keep, 0.0)
+            for b in range(3):
+                inside = jnp.where((col + (b - 1) >= 0) & (col + (b - 1) < cols), keep, 0.0)
+                mask_rows[d, t * 3 + b] = inside
+
+    def turn(g, d, got):
+        v = got[d].astype(F32)[0:part]
+        for t in range(3):
+            for b in range(3):
+                shift = t * cols - (b - 1)
+                moved = v if shift == 0 else pltpu.roll(v, shift % lanes, 1)
+                if t > 0 or b != 1:
+                    keep = mask_rows[d, t * 3 + b]
+                    moved = moved * jnp.concatenate([keep] * (part // 8), axis=0)
+                middle = pltpu.roll(moved, lanes - slab, 1)
+                low = moved[:, 0:cells].astype(BF16)
+                mid = middle[:, 0:cells].astype(BF16)
+                high = moved[:, 2 * slab :].astype(BF16)
+                for a, w in enumerate((low, mid, high)):
+                    at = ((t * 3 + a) * 3 + b) * part
+                    turned[g, d, at : at + part, :] = w
+
+    def partial_sum(g, d, right, fresh):
+        term = jnp.dot(turned[g, d], right, preferred_element_type=F32)
+        flat[g] = term if fresh else flat[g] + term
 
     def step_b(g):
         wait(copies_a(g))
         for k in range(n_z):
-            own = flats[g][pl.ds(pl.multiple_of((2 * k + core) * share, 8), share), :]
-            sum_a[g, k, 0:share, :] = own + recv_a[g, k, 0:share].astype(F32)
-        for i in range(1, n_dp):
-            send_b[g, i - 1] = sum_a[g, :, part(lax.rem(dp + i, n_dp)), :].astype(BF16)
-        start(copies_b(g))
+            sum_a[g, k] = flat[g, window(2 * k + core), :] + recv_a[g, k]
+        for j in range(1, n_z):
+            send_c[g, j - 1] = sum_a[g, lax.rem(z + j, n_z)].astype(BF16)
+        start(copies_c(g))
 
     def step_c(g):
-        wait(copies_b(g))
-        total = sum_a[g, :, part(dp), :]
-        for i in range(1, n_dp):
-            total = total + recv_b[g, i - 1].astype(F32)
-        sum_b[g] = total
-        for j in range(1, n_z):
-            send_c[g, j - 1] = sum_b[g, lax.rem(z + j, n_z)].astype(BF16)
-        start(copies_c(g))
-
-    def step_d(g):
         wait(copies_c(g))
-        total = sum_b[g, z]
+        total = sum_a[g, z]
         for j in range(1, n_z):
             total = total + recv_c[g, j - 1].astype(F32)
-        fin[g, part(dp), :] = total * scale
+        every[g, dp] = (total * scale).astype(BF16)
         start(copies_d(g))
 
-    def step_a(g):
-        for k, copy in enumerate(copies_a(g)):
-            at = pl.ds(pl.multiple_of((2 * k + 1 - core) * share, 8), share)
-            send_a[g, k, 0:share, :] = flats[g][at, :].astype(BF16)
-            copy.start()
+    def step_d(g):
+        wait(copies_d(g))
+        for q in range(n_dp):
+            v = every[g, q].astype(F32)
+            for i in range(n_tap):
+                at = i * ch + q * quarter
+                spread[g, at : at + quarter, :] = v[i * part : i * part + quarter]
+        at = pl.multiple_of(share * tile - ch * tap_0(tile), 8)
+        out_v[g] = spread[g, pl.ds(at, share), :]
+        copy = pltpu.make_async_copy(out_v.at[g], outs[g], out_sem.at[g])
+        copy.start()
+        return copy
 
     hidden = edges(first * sigma)
-    fill_columns(cols_h, four(hidden), same, False)
-    g_own = g_all[2 : 2 + rows].reshape(rows * slab, ch)
-    kernel_grad(flat2, cols_h, 0, g_own.astype(BF16))
-    step_a(1)
+    deal(hidden, hid_out, hid_got, copies_hid)
+    g_own = g_all[2 : 2 + rows].reshape(cells, ch)
     fill_columns(cols_g, four(g_all), same, True)
     hidden_grad = conv_dots(cols_g, w2t, 0, wide, slab, True)
     act = edges(hidden_grad * sigma * (1.0 + first * (1.0 - sigma)))
-    act_own = act[1 : 1 + rows].reshape(rows * slab, ch).astype(BF16)
-
+    act_got[dp] = act[1 : 1 + rows].reshape(cells, ch).astype(BF16)
+    start(copies_act)
+
+    wait(copies_seg)
+    for d in range(n_dp):
+        make_masks(d)
+    wait(copies_cot)
+    for d in range(n_dp):
+        v = (cot_got[d].astype(F32) * 0.25).reshape(cells // 4, ch)
+        g_tmp[pl.ds(0, cells // 4, stride=2), :] = v
+        g_tmp[pl.ds(1, cells // 4, stride=2), :] = v
+        v = g_tmp[0 : cells // 2, :].astype(BF16).reshape(rows // 2, slab, ch)
+        g_got[d] = jnp.stack([v, v], axis=1).reshape(cells, ch)
+    wait(copies_x)
+    for d in range(n_dp):
+        turn(0, d, x_got)
+    fill_columns(cols_h, four(hidden), same, False)
+    for i in range(n_dp):
+        if i > 0:
+            copies_hid[i - 1].wait()
+        turn(1, sender(i), hid_got)
+        partial_sum(1, sender(i), g_got[sender(i)], i == 0)
+    start(copies_a(1))
+    for i in range(n_dp):
+        if i > 0:
+            copies_act[i - 1].wait()
+        partial_sum(0, sender(i), act_got[sender(i)], i == 0)
+    start(copies_a(0))
     step_b(1)
-    kernel_grad(flat1, cols_x, 1, act_own)
-    step_a(0)
-    fill_columns(cols_a, four(act), same, True)
     step_b(0)
+
     second = conv_dots(cols_h, w2, 0, rows, slab, False)
     summed = mine.reshape(rows, slab, ch) + second.reshape(rows, slab, ch)
     pairs = rows // 2
@@ -343,24 +410,18 @@
             )
     put_pooled = pltpu.make_async_copy(pooled, pooled_hbm.at[0], out_sem.at[2])
     put_pooled.start()
-    step_c(1)
+    fill_columns(cols_a, four(act), same, True)
     back = conv_dots(cols_a, w1t, 0, rows, slab, True)
     total = (g_own + back).reshape(rows, frames, cols, ch)
     for r in range(rows):
         in_grad[:, r] = total[r]
     put_grad = pltpu.make_async_copy(in_grad, in_grad_hbm.at[0], out_sem.at[3])
     put_grad.start()
+    step_c(1)
     step_c(0)
-    step_d(1)
-    step_d(0)
-    puts = [pltpu.make_async_copy(fin.at[g, 0:share], outs[g], out_sem.at[g]) for g in range(2)]
-    for g in (1, 0):
-        wait(copies_d(g))
-        puts[g].start()
-    put_pooled.wait()
-    put_grad.wait()
-    for g in (1, 0):
-        puts[g].wait()
+    puts = [put_pooled, put_grad, step_d(1), step_d(0)]
+    for copy in puts:
+        copy.wait()
 
 
 def hand_out(*refs):
@@ -381,11 +442,14 @@
     slab = frames * cols
     taps = weight_first.shape[0]
     share = taps // n_tile
-    chunk = up16(-(-share // n_dp))
     n_z = n_tile // 2
+    quarter = ch // n_dp
+    part = up16(quarter)
+    n_tap = max(-(-share * (k + 1) // ch) - share * k // ch for k in range(n_tile))
     scale = 1.0 / math.sqrt(n_dp * n_tile * rows * slab)
     vmem = pl.BlockSpec(memory_space=pltpu.VMEM)
     cells = rows * slab
+    lanes = (rows + 2) * slab
     sem = pltpu.SemaphoreType.DMA
     anywhere = pl.BlockSpec(memory_space=pltpu.HBM)
     shapes = (
@@ -395,7 +459,7 @@
         jax.ShapeDtypeStruct((share, ch), F32),
     )
     results = pl.pallas_call(
-        functools.partial(kernel, (n_tile, n_dp, share, chunk, scale)),
+        functools.partial(kernel, (n_tile, n_dp, share, quarter, part, n_tap, scale)),
         out_shape=shapes,
         in_specs=[pl.BlockSpec(memory_space=pltpu.SMEM)] + [anywhere] * 4,
         out_specs=(anywhere,) * 4,
@@ -418,20 +482,31 @@
             pltpu.VMEM((taps, ch), BF16),
             pltpu.VMEM((taps, ch), BF16),
             pltpu.VMEM((cells // 2, ch), F32),
-            pltpu.VMEM((taps, ch), F32),
-            pltpu.VMEM((taps, ch), F32),
-            pltpu.VMEM((2, n_z, up16(share), ch), BF16),
-            pltpu.VMEM((2, n_z, up16(share), ch), BF16),
-            pltpu.VMEM((2, n_z, n_dp * chunk, ch), F32),
-            pltpu.VMEM((2, n_dp - 1, n_z, chunk, ch), BF16),
-            pltpu.VMEM((2, n_dp - 1, n_z, chunk, ch), BF16),
-            pltpu.VMEM((2, n_z, chunk, ch), F32),
-            pltpu.VMEM((2, n_z - 1, chunk, ch), BF16),
-            pltpu.VMEM((2, n_z - 1, chunk, ch), BF16),
-            pltpu.VMEM((2, n_dp * chunk, ch), F32),
+            pltpu.VMEM((n_dp, 16, lanes), BF16),
+            pltpu.VMEM((n_dp, 9, 8, lanes), F32),
+            pltpu.VMEM((n_dp, part, lanes), BF16),
+            pltpu.VMEM((n_dp, part, lanes), BF16),
+            pltpu.VMEM((n_dp, part, lanes), BF16),
+            pltpu.VMEM((n_dp, part, lanes), BF16),
+            pltpu.VMEM((n_dp, rows // 2, frames, cols // 2, ch), BF16),
+            pltpu.VMEM((n_dp, cells, ch), BF16),
+            pltpu.VMEM((n_dp, cells, ch), BF16),
+            pltpu.VMEM((2, n_dp, taps // ch * part, cells), BF16),
+            pltpu.VMEM((2, taps // ch * part, ch), F32),
+            pltpu.VMEM((2, n_z, n_tap * part, ch), F32),
+            pltpu.VMEM((2, n_z, n_tap * part, ch), F32),
+            pltpu.VMEM((2, n_z - 1, n_tap * part, ch), BF16),
+            pltpu.VMEM((2, n_z - 1, n_tap * part, ch), BF16),
+            pltpu.VMEM((2, n_dp, n_tap * part, ch), BF16),
+            pltpu.VMEM((2, n_tap * ch, ch), F32),
+            pltpu.VMEM((2, share, ch), F32),
             sem((4,)), sem((4,)),
+            sem((n_dp - 1,)), sem((n_dp - 1,)),
+            sem((n_dp - 1,)), sem((n_dp - 1,)),
+            sem((n_dp - 1,)), sem((n_dp - 1,)),
+            sem((n_dp - 1,)), sem((n_dp - 1,)),
+            sem((n_dp - 1,)), sem((n_dp - 1,)),
             sem((2, n_z)), sem((2, n_z)),
-            sem((2, n_dp - 1)), sem((2, n_dp - 1)),
             sem((2, n_z - 1)), sem((2, n_z - 1)),
             sem((2, n_dp - 1)), sem((2, n_dp - 1)),
         ],

time: 36.4 us -> 34.6 us (0.951)
  Pallas kernels: 35.6 us -> 33.8 us
    pallas_call x1, Pallas kernels: 33.7 us -> 31.8 us  [local(): pl.pallas_call(functools.partial(kernel, (n_tile, n_dp, share, quarter, p...]
where the time goes in v2:
time: 34.6 us; the launch traced here: 34.4 us
  Pallas kernels  33.8 us (98%)
  between operations  0.64 us (2%)
    pallas_call x1, Pallas kernels, local(): pl.pallas_call(functools.partial(kernel, (n_tile, n_dp, share, quarter, p...  31.8 us
    pallas_call x1, Pallas kernels, local(): pl.pallas_call(hand_out, out_shape=shapes, in_specs=[pl.BlockSpec(memory_...  1.93 us

profile of v2, /device:TPU:0, one launch (start us, length us, event | category | flops | bytes accessed | tf_op | source)
XLA Modules:
  0.0 34.4 jit_solution(2577580097963726491)
XLA Ops:
  0.6 31.8 %shard_map.84 = (f32[1,8,2,4,128]{4,3,2,1,0:T(4,128)}, f32[1,8,4,8,128]{4,3,2,1,0:T(8,128)}, f32[432,128]{1,0:T(8,128)}, f32[432,128]{1,0:T(8,128)}) custom-call(s32[1,8]{1,0:T(1,128)} %seg.1, bf16[1,8,4,8,128]{4,3,2,1,0:T(8,128)(2,1)} %x_hbm.1, bf16[3456,128]{1,0:T(8,128)(2,1)} %w1_hbm.1, bf16[3456,128]{1,0:T(8,128)(2,1)} %w2_hbm.1, ...), custom_call_target="tpu_custom_call" | custom-call | tf_op jit(solution)/shard_map/pallas_call | solution.py:461
  32.5 1.9 %shard_map.85 = (f32[1,8,2,4,128]{4,3,2,1,0:T(4,128)}, f32[1,8,4,8,128]{4,3,2,1,0:T(8,128)}, f32[432,128]{1,0:T(8,128)}, f32[432,128]{1,0:T(8,128)}) custom-call(f32[1,8,2,4,128]{4,3,2,1,0:T(4,128)} %get-tuple-element.8.refs_0_, f32[1,8,4,8,128]{4,3,2,1,0:T(8,128)} %get-tuple-element.9.refs_1_, f32[432,128]{1,0:T(8,128)} %get-tuple-element.10.refs_2_, ...), custom_call_target="tpu_custom_call" | custom-call | tf_op jit(solution)/shard_map/pallas_call | solution.py:518

commit v3 on v2

--- a/solution.py
+++ b/solution.py
@@ -72,7 +72,7 @@
     h_send, h_recv, x_send, x_recv, s_send, s_recv, k_send, k_recv, g_send, g_recv, t_send, t_recv,
     a_send, a_recv, c_send, c_recv, d_send, d_recv,
 ):
-    n_tile, n_dp, share, quarter, part, n_tap, scale = cfg
+    n_tile, n_dp, share, quarter, part, unit, n_unit, scale = cfg
     n_z = n_tile // 2
     rows, frames, cols, ch = x_in.shape
     slab = frames * cols
@@ -85,7 +85,10 @@
     wide = rows + 2
     cells = rows * slab
     lanes = wide * slab
-    block = n_tap * part
+    per_tap, per_quarter = ch // unit, quarter // unit
+    slot = part // per_quarter
+    margin = (spread.shape[1] - share) // 2
+    block = n_unit * slot
 
     load_x = [
         pltpu.make_async_copy(x_hbm.at[0, :, r], x_in.at[r], in_sem.at[2 + r]) for r in range(rows)
@@ -128,9 +131,9 @@
     if part > quarter:
         x_out[:, quarter:, :] = jnp.zeros((n_dp, part - quarter, lanes), BF16)
         hid_out[:, quarter:, :] = jnp.zeros((n_dp, part - quarter, lanes), BF16)
-    lane = lax.broadcasted_iota(jnp.int32, (16, lanes), 1)
+    lane = lax.broadcasted_iota(jnp.int32, (16, 2 * slab), 1)
     frame = lax.rem(lax.div(lane, cols), frames)
-    number = jnp.zeros((16, lanes), F32)
+    number = jnp.zeros((16, 2 * slab), F32)
     for f in range(frames):
         number = jnp.where(frame == f, seg[0, f].astype(F32), number)
     seg_rows[dp] = number.astype(BF16)
@@ -203,6 +206,19 @@
     start(copies_seg)
     cot_got[dp] = c_in[...]
 
+    def deal(v, out, at):
+        v = v.reshape(-1, ch).T.astype(BF16)
+        for q in range(n_dp):
+            out[q, 0:quarter, at : at + v.shape[1]] = v[q * quarter : (q + 1) * quarter]
+
+    mine = x_in[...].astype(F32)
+    deal(mine, x_out, 0)
+    copies_x = [
+        to_dp(lambda q: x_out.at[q, :, 0:cells], x_got.at[dp, :, 0:cells], x_send.at[0], x_recv.at[0]),
+        to_dp(lambda q: x_out.at[q, :, cells:], x_got.at[dp, :, cells:], x_send.at[1], x_recv.at[1]),
+    ]
+    start(copies_x[0])
+
     load_w1.wait()
     load_w2.wait()
     flip(w2, w2t)
@@ -231,20 +247,13 @@
     def four(v):
         return v.reshape(v.shape[0], frames, cols, ch)
 
-    mine = x_in[...].astype(F32)
     x_all = jnp.concatenate([x_halo[0].astype(F32), mine, x_halo[1].astype(F32)], axis=0)
-    copies_x = to_dp(lambda q: x_out.at[q], x_got.at[dp], x_send, x_recv)
     copies_hid = to_dp(lambda q: hid_out.at[q], hid_got.at[dp], t_send, t_recv)
     copies_act = to_dp(lambda q: act_got.at[dp], act_got.at[dp], g_send, g_recv)
 
-    def deal(v, out, got, copies):
-        v = v.reshape(lanes, ch).T.astype(BF16)
-        for q in range(n_dp):
-            out[q, 0:quarter, :] = v[q * quarter : (q + 1) * quarter]
-        start(copies)
-        got[dp] = out[dp]
-
-    deal(x_all[1 : 1 + wide], x_out, x_got, copies_x)
+    deal(jnp.concatenate([x_all[wide : wide + 1], x_all[1:2]], axis=0), x_out, cells)
+    start(copies_x[1])
+    x_got[dp] = x_out[dp]
     fill_columns(cols_x, x_all, same, False)
     c_all = jnp.concatenate([g_halo[0], c_in[...], g_halo[1]], axis=0).astype(F32) * 0.25
     half = (g_rows + 2) * slab // 2
@@ -263,11 +272,13 @@
         v = v.reshape(wide, slab, ch)
         return jnp.concatenate([v[:1] * top, v[1:-1], v[-1:] * low], axis=0)
 
-    def tap_0(to):
-        return jnp.minimum(lax.div(share * to, ch), taps - n_tap)
+    def first_unit(to, q):
+        unit_at = lax.div(share, unit) * to
+        beyond = jnp.clip(lax.rem(unit_at, per_tap) - per_quarter * q, 0, per_quarter)
+        return jnp.minimum(per_quarter * lax.div(unit_at, per_tap) + beyond, taps * per_quarter - n_unit)
 
     def window(to):
-        return pl.ds(pl.multiple_of(tap_0(to) * part, 16), block)
+        return pl.ds(pl.multiple_of(first_unit(to, dp) * slot, 16), block)
 
     def copies_a(g):
         return [
@@ -297,11 +308,11 @@
 
     def make_masks(d):
         number = seg_rows[d].astype(F32)[0:8]
-        at = lax.broadcasted_iota(jnp.int32, (8, lanes), 1)
+        at = lax.broadcasted_iota(jnp.int32, (8, 2 * slab), 1)
         when = lax.rem(lax.div(at, cols), frames)
         col = lax.rem(at, cols)
         for t in range(3):
-            keep = jnp.ones((8, lanes), F32)
+            keep = jnp.ones((8, 2 * slab), F32)
             if t > 0:
                 keep = jnp.where(number == pltpu.roll(number, t * cols, 1), 1.0, 0.0)
                 keep = jnp.where(when >= t, keep, 0.0)
@@ -316,15 +327,12 @@
                 shift = t * cols - (b - 1)
                 moved = v if shift == 0 else pltpu.roll(v, shift % lanes, 1)
                 if t > 0 or b != 1:
-                    keep = mask_rows[d, t * 3 + b]
+                    keep = jnp.concatenate([mask_rows[d, t * 3 + b]] * (wide // 2), axis=1)
                     moved = moved * jnp.concatenate([keep] * (part // 8), axis=0)
-                middle = pltpu.roll(moved, lanes - slab, 1)
-                low = moved[:, 0:cells].astype(BF16)
-                mid = middle[:, 0:cells].astype(BF16)
-                high = moved[:, 2 * slab :].astype(BF16)
-                for a, w in enumerate((low, mid, high)):
+                for a in range(3):
+                    w = moved if a == 1 else pltpu.roll(moved, (1 - a) * slab % lanes, 1)
                     at = ((t * 3 + a) * 3 + b) * part
-                    turned[g, d, at : at + part, :] = w
+                    turned[g, d, at : at + part, :] = w[:, 0:cells].astype(BF16)
 
     def partial_sum(g, d, right, fresh):
         term = jnp.dot(turned[g, d], right, preferred_element_type=F32)
@@ -350,17 +358,21 @@
         wait(copies_d(g))
         for q in range(n_dp):
             v = every[g, q].astype(F32)
-            for i in range(n_tap):
-                at = i * ch + q * quarter
-                spread[g, at : at + quarter, :] = v[i * part : i * part + quarter]
-        at = pl.multiple_of(share * tile - ch * tap_0(tile), 8)
-        out_v[g] = spread[g, pl.ds(at, share), :]
+            for i in range(n_unit):
+                u = first_unit(tile, q) + i
+                at = ch * lax.div(u, per_quarter) + unit * lax.rem(u, per_quarter) + quarter * q - share * tile
+                at = pl.multiple_of(at + margin, 8)
+                spread[g, pl.ds(at, unit), :] = v[i * slot : i * slot + unit]
+        out_v[g] = spread[g, margin : margin + share, :]
         copy = pltpu.make_async_copy(out_v.at[g], outs[g], out_sem.at[g])
         copy.start()
         return copy
 
     hidden = edges(first * sigma)
-    deal(hidden, hid_out, hid_got, copies_hid)
+    by_row = hidden.reshape(wide, slab, ch)
+    deal(jnp.concatenate([by_row[1:], by_row[:1]], axis=0), hid_out, 0)
+    start(copies_hid)
+    hid_got[dp] = hid_out[dp]
     g_own = g_all[2 : 2 + rows].reshape(cells, ch)
     fill_columns(cols_g, four(g_all), same, True)
     hidden_grad = conv_dots(cols_g, w2t, 0, wide, slab, True)
@@ -378,7 +390,8 @@
         g_tmp[pl.ds(1, cells // 4, stride=2), :] = v
         v = g_tmp[0 : cells // 2, :].astype(BF16).reshape(rows // 2, slab, ch)
         g_got[d] = jnp.stack([v, v], axis=1).reshape(cells, ch)
-    wait(copies_x)
+    wait(copies_x[0])
+    wait(copies_x[1])
     for d in range(n_dp):
         turn(0, d, x_got)
     fill_columns(cols_h, four(hidden), same, False)
@@ -445,7 +458,16 @@
     n_z = n_tile // 2
     quarter = ch // n_dp
     part = up16(quarter)
-    n_tap = max(-(-share * (k + 1) // ch) - share * k // ch for k in range(n_tile))
+    unit = math.gcd(share, quarter)
+    per_quarter = quarter // unit
+
+    def before(to, q):
+        whole, rest = divmod(share // unit * to, ch // unit)
+        return per_quarter * whole + min(max(rest - per_quarter * q, 0), per_quarter)
+
+    n_unit = max(before(k + 1, q) - before(k, q) for k in range(n_tile) for q in range(n_dp))
+    block = n_unit * (part // per_quarter)
+    span = share + 2 * ch * (n_unit // per_quarter + 2)
     scale = 1.0 / math.sqrt(n_dp * n_tile * rows * slab)
     vmem = pl.BlockSpec(memory_space=pltpu.VMEM)
     cells = rows * slab
@@ -459,7 +481,7 @@
         jax.ShapeDtypeStruct((share, ch), F32),
     )
     results = pl.pallas_call(
-        functools.partial(kernel, (n_tile, n_dp, share, quarter, part, n_tap, scale)),
+        functools.partial(kernel, (n_tile, n_dp, share, quarter, part, unit, n_unit, scale)),
         out_shape=shapes,
         in_specs=[pl.BlockSpec(memory_space=pltpu.SMEM)] + [anywhere] * 4,
         out_specs=(anywhere,) * 4,
@@ -482,8 +504,8 @@
             pltpu.VMEM((taps, ch), BF16),
             pltpu.VMEM((taps, ch), BF16),
             pltpu.VMEM((cells // 2, ch), F32),
-            pltpu.VMEM((n_dp, 16, lanes), BF16),
-            pltpu.VMEM((n_dp, 9, 8, lanes), F32),
+            pltpu.VMEM((n_dp, 16, 2 * slab), BF16),
+            pltpu.VMEM((n_dp, 9, 8, 2 * slab), F32),
             pltpu.VMEM((n_dp, part, lanes), BF16),
             pltpu.VMEM((n_dp, part, lanes), BF16),
             pltpu.VMEM((n_dp, part, lanes), BF16),
@@ -493,15 +515,15 @@
             pltpu.VMEM((n_dp, cells, ch), BF16),
             pltpu.VMEM((2, n_dp, taps // ch * part, cells), BF16),
             pltpu.VMEM((2, taps // ch * part, ch), F32),
-            pltpu.VMEM((2, n_z, n_tap * part, ch), F32),
-            pltpu.VMEM((2, n_z, n_tap * part, ch), F32),
-            pltpu.VMEM((2, n_z - 1, n_tap * part, ch), BF16),
-            pltpu.VMEM((2, n_z - 1, n_tap * part, ch), BF16),
-            pltpu.VMEM((2, n_dp, n_tap * part, ch), BF16),
-            pltpu.VMEM((2, n_tap * ch, ch), F32),
+            pltpu.VMEM((2, n_z, block, ch), F32),
+            pltpu.VMEM((2, n_z, block, ch), F32),
+            pltpu.VMEM((2, n_z - 1, block, ch), BF16),
+            pltpu.VMEM((2, n_z - 1, block, ch), BF16),
+            pltpu.VMEM((2, n_dp, block, ch), BF16),
+            pltpu.VMEM((2, span, ch), F32),
             pltpu.VMEM((2, share, ch), F32),
             sem((4,)), sem((4,)),
-            sem((n_dp - 1,)), sem((n_dp - 1,)),
+            sem((2, n_dp - 1)), sem((2, n_dp - 1)),
             sem((n_dp - 1,)), sem((n_dp - 1,)),
             sem((n_dp - 1,)), sem((n_dp - 1,)),
             sem((n_dp - 1,)), sem((n_dp - 1,)),

time: 34.6 us -> 32.5 us (0.939)
  Pallas kernels: 33.8 us -> 31.7 us
    pallas_call x1, Pallas kernels: 31.8 us -> 29.8 us  [local(): pl.pallas_call(functools.partial(kernel, (n_tile, n_dp, share, quarter, p...]
where the time goes in v3:
time: 32.5 us; the launch traced here: 32.4 us
  Pallas kernels  31.7 us (98%)
  between operations  0.64 us (2%)
    pallas_call x1, Pallas kernels, local(): pl.pallas_call(functools.partial(kernel, (n_tile, n_dp, share, quarter, p...  29.8 us
    pallas_call x1, Pallas kernels, local(): pl.pallas_call(hand_out, out_shape=shapes, in_specs=[pl.BlockSpec(memory_...  1.93 us

profile of v3, /device:TPU:0, one launch (start us, length us, event | category | flops | bytes accessed | tf_op | source)
XLA Modules:
  0.0 32.4 jit_solution(3986303082317362793)
XLA Ops:
  0.6 29.8 %shard_map.84 = (f32[1,8,2,4,128]{4,3,2,1,0:T(4,128)}, f32[1,8,4,8,128]{4,3,2,1,0:T(8,128)}, f32[432,128]{1,0:T(8,128)}, f32[432,128]{1,0:T(8,128)}) custom-call(s32[1,8]{1,0:T(1,128)} %seg.1, bf16[1,8,4,8,128]{4,3,2,1,0:T(8,128)(2,1)} %x_hbm.1, bf16[3456,128]{1,0:T(8,128)(2,1)} %w1_hbm.1, bf16[3456,128]{1,0:T(8,128)(2,1)} %w2_hbm.1, ...), custom_call_target="tpu_custom_call" | custom-call | tf_op jit(solution)/shard_map/pallas_call | solution.py:483
  30.4 1.9 %shard_map.85 = (f32[1,8,2,4,128]{4,3,2,1,0:T(4,128)}, f32[1,8,4,8,128]{4,3,2,1,0:T(8,128)}, f32[432,128]{1,0:T(8,128)}, f32[432,128]{1,0:T(8,128)}) custom-call(f32[1,8,2,4,128]{4,3,2,1,0:T(4,128)} %get-tuple-element.8.refs_0_, f32[1,8,4,8,128]{4,3,2,1,0:T(8,128)} %get-tuple-element.9.refs_1_, f32[432,128]{1,0:T(8,128)} %get-tuple-element.10.refs_2_, ...), custom_call_target="tpu_custom_call" | custom-call | tf_op jit(solution)/shard_map/pallas_call | solution.py:540

commit v4 on v3

--- a/solution.py
+++ b/solution.py
@@ -65,10 +65,10 @@
 def kernel(
     cfg,
     seg, x_hbm, w1_hbm, w2_hbm, c_hbm,
-    pooled_hbm, in_grad_hbm, out1, out2,
-    pooled, in_grad, out_sem, x_in, w1, w2, c_in, g_tmp, in_sem, x_halo, g_halo, cols_x, cols_h, cols_g, cols_a, w1t, w2t, pool_tmp,
+    pooled, in_grad, out1, out2,
+    x_in, w1, w2, c_in, g_tmp, in_sem, x_halo, g_halo, cols_x, cols_h, cols_g, cols_a, w1t, w2t, pool_tmp,
     seg_rows, mask_rows, x_out, x_got, hid_out, hid_got, cot_got, act_got, g_got, turned, flat,
-    recv_a, sum_a, send_c, recv_c, every, spread, out_v,
+    recv_a, sum_a, send_c, recv_c, every, spread,
     h_send, h_recv, x_send, x_recv, s_send, s_recv, k_send, k_recv, g_send, g_recv, t_send, t_recv,
     a_send, a_recv, c_send, c_recv, d_send, d_recv,
 ):
@@ -363,10 +363,7 @@
                 at = ch * lax.div(u, per_quarter) + unit * lax.rem(u, per_quarter) + quarter * q - share * tile
                 at = pl.multiple_of(at + margin, 8)
                 spread[g, pl.ds(at, unit), :] = v[i * slot : i * slot + unit]
-        out_v[g] = spread[g, margin : margin + share, :]
-        copy = pltpu.make_async_copy(out_v.at[g], outs[g], out_sem.at[g])
-        copy.start()
-        return copy
+        outs[g][...] = spread[g, margin : margin + share, :]
 
     hidden = edges(first * sigma)
     by_row = hidden.reshape(wide, slab, ch)
@@ -417,36 +414,27 @@
     for i in range(pairs):
         for f in range(frames):
             at = i * slab + f * cols
-            pooled[f, i] = 0.25 * (
+            pooled[0, f, i] = 0.25 * (
                 pool_tmp[pl.ds(at, cols // 2, stride=2), :]
                 + pool_tmp[pl.ds(at + 1, cols // 2, stride=2), :]
             )
-    put_pooled = pltpu.make_async_copy(pooled, pooled_hbm.at[0], out_sem.at[2])
-    put_pooled.start()
     fill_columns(cols_a, four(act), same, True)
     back = conv_dots(cols_a, w1t, 0, rows, slab, True)
     total = (g_own + back).reshape(rows, frames, cols, ch)
     for r in range(rows):
-        in_grad[:, r] = total[r]
-    put_grad = pltpu.make_async_copy(in_grad, in_grad_hbm.at[0], out_sem.at[3])
-    put_grad.start()
+        in_grad[0, :, r] = total[r]
     step_c(1)
     step_c(0)
-    puts = [put_pooled, put_grad, step_d(1), step_d(0)]
-    for copy in puts:
-        copy.wait()
+    step_d(1)
+    step_d(0)
 
 
 def hand_out(*refs):
-    held, load_sem, store_sem = refs[8:12], refs[12], refs[13]
-    loads = [pltpu.make_async_copy(refs[i], held[i], load_sem.at[i]) for i in range(4)]
-    stores = [pltpu.make_async_copy(held[i], refs[4 + i], store_sem.at[i]) for i in range(4)]
-    for copy in loads:
+    sems = refs[8]
+    copies = [pltpu.make_async_copy(refs[i], refs[4 + i], sems.at[i]) for i in (1, 2, 3, 0)]
+    for copy in copies:
         copy.start()
-    for i in (0, 2, 3, 1):
-        loads[i].wait()
-        stores[i].start()
-    for copy in stores:
+    for copy in copies:
         copy.wait()
 
 
@@ -480,15 +468,16 @@
         jax.ShapeDtypeStruct((share, ch), F32),
         jax.ShapeDtypeStruct((share, ch), F32),
     )
+    held = [
+        pltpu.with_memory_space_constraint(v, pltpu.HBM)
+        for v in (segments, clip_frames, weight_first, weight_second, cotangent)
+    ]
     results = pl.pallas_call(
         functools.partial(kernel, (n_tile, n_dp, share, quarter, part, unit, n_unit, scale)),
         out_shape=shapes,
         in_specs=[pl.BlockSpec(memory_space=pltpu.SMEM)] + [anywhere] * 4,
-        out_specs=(anywhere,) * 4,
+        out_specs=(vmem,) * 4,
         scratch_shapes=[
-            pltpu.VMEM((frames, rows // 2, cols // 2, ch), F32),
-            pltpu.VMEM((frames, rows, cols, ch), F32),
-            sem((4,)),
             pltpu.VMEM((rows, frames, cols, ch), BF16),
             pltpu.VMEM((taps, ch), BF16),
             pltpu.VMEM((taps, ch), BF16),
@@ -521,7 +510,6 @@
             pltpu.VMEM((2, n_z - 1, block, ch), BF16),
             pltpu.VMEM((2, n_dp, block, ch), BF16),
             pltpu.VMEM((2, span, ch), F32),
-            pltpu.VMEM((2, share, ch), F32),
             sem((4,)), sem((4,)),
             sem((2, n_dp - 1)), sem((2, n_dp - 1)),
             sem((n_dp - 1,)), sem((n_dp - 1,)),
@@ -533,16 +521,17 @@
             sem((2, n_dp - 1)), sem((2, n_dp - 1)),
         ],
         compiler_params=pltpu.CompilerParams(
-            collective_id=0, has_side_effects=True, vmem_limit_bytes=60 * 1024 * 1024
+            collective_id=0, has_side_effects=True, vmem_limit_bytes=50 * 1024 * 1024
         ),
-    )(segments, clip_frames, weight_first, weight_second, cotangent)
+    )(*held)
     return tuple(
         pl.pallas_call(
             hand_out,
             out_shape=shapes,
             in_specs=[pl.BlockSpec(memory_space=pl.ANY)] * 4,
             out_specs=(pl.BlockSpec(memory_space=pl.ANY),) * 4,
-            scratch_shapes=[pltpu.VMEM(v.shape, v.dtype) for v in shapes] + [sem((4,))] * 2,
+            scratch_shapes=[sem((4,))],
+            compiler_params=pltpu.CompilerParams(vmem_limit_bytes=4 * 1024 * 1024),
         )(*results)
     )
 

time: 32.5 us -> 30.7 us (0.945)
  Pallas kernels: 31.7 us -> 29.9 us
    pallas_call x1, Pallas kernels: 1.93 us -> 0.84 us  [local(): pl.pallas_call(hand_out, out_shape=shapes, in_specs=[pl.BlockSpec(memory_...]
    pallas_call x1, Pallas kernels: 29.8 us -> 29.1 us  [local(): pl.pallas_call(functools.partial(kernel, (n_tile, n_dp, share, quarter, p...]
where the time goes in v4:
time: 30.7 us; the launch traced here: 30.6 us
  Pallas kernels  29.9 us (97%)
  between operations  0.64 us (2%)
    pallas_call x1, Pallas kernels, local(): pl.pallas_call(functools.partial(kernel, (n_tile, n_dp, share, quarter, p...  29.1 us
    pallas_call x1, Pallas kernels, local(): pl.pallas_call(hand_out, out_shape=shapes, in_specs=[pl.BlockSpec(memory_...  0.84 us

profile of v4, /device:TPU:0, one launch (start us, length us, event | category | flops | bytes accessed | tf_op | source)
XLA Modules:
  0.0 30.6 jit_solution(8375914546223022775)
XLA Ops:
  0.6 29.1 %shard_map.84 = (f32[1,8,2,4,128]{4,3,2,1,0:T(4,128)S(1)}, f32[1,8,4,8,128]{4,3,2,1,0:T(8,128)S(1)}, f32[432,128]{1,0:T(8,128)S(1)}, f32[432,128]{1,0:T(8,128)S(1)}) custom-call(s32[1,8]{1,0:T(1,128)} %seg.1, bf16[1,8,4,8,128]{4,3,2,1,0:T(8,128)(2,1)} %x_hbm.1, bf16[3456,128]{1,0:T(8,128)(2,1)} %w1_hbm.1, bf16[3456,128]{1,0:T(8,128)(2,1)} %w2_hbm.1, ...), custom_call_target="tpu_custom_call" | custom-call | tf_op jit(solution)/shard_map/pallas_call | solution.py:475
  29.7 0.8 %shard_map.85 = (f32[1,8,2,4,128]{4,3,2,1,0:T(4,128)}, f32[1,8,4,8,128]{4,3,2,1,0:T(8,128)}, f32[432,128]{1,0:T(8,128)}, f32[432,128]{1,0:T(8,128)}) custom-call(f32[1,8,2,4,128]{4,3,2,1,0:T(4,128)S(1)} %get-tuple-element.8.refs_0_, f32[1,8,4,8,128]{4,3,2,1,0:T(8,128)S(1)} %get-tuple-element.9.refs_1_, f32[432,128]{1,0:T(8,128)S(1)} %get-tuple-element.10.refs_2_, ...), custom_call_target="tpu_custom_call" | custom-call | tf_op jit(solution)/shard_map/pallas_call | solution.py:528

commit v5 on v4

--- a/solution.py
+++ b/solution.py
@@ -27,7 +27,7 @@
     return jnp.where(keep, moved, 0.0)
 
 
-def fill_columns(dst, cells, same, reverse):
+def fill_columns(dst, cells, same, reverse, first=0):
     rows, frames, cols, ch = cells.shape
     for ci in range(3):
         moved = shifted_cols(cells, (1 - ci) if reverse else (ci - 1))
@@ -44,7 +44,8 @@
                     parts.append(moved[:, src] * same[t][max(f, src)])
             block = jnp.stack(parts, axis=1).reshape(rows * frames * cols, ch)
             at = (t * 3 + ci) * ch
-            dst[:, at : at + ch] = block.astype(BF16)
+            from_row = first * frames * cols
+            dst[from_row : from_row + rows * frames * cols, at : at + ch] = block.astype(BF16)
 
 
 def conv_dots(cols_ref, w_ref, start, rows, slab, reverse):
@@ -62,14 +63,67 @@
     return acc
 
 
+def own_dots(cols_ref, w_ref, rows, slab, reverse):
+    total = None
+    span = w_ref.shape[1] * 3
+    for a in range(3):
+        e = 2 - a if reverse else a
+        term = None
+        for t in range(3):
+            one = jnp.dot(
+                cols_ref[2 * slab : (2 + rows) * slab, t * span : (t + 1) * span],
+                w_ref[(t * 3 + a) * span : (t * 3 + a + 1) * span, :],
+                preferred_element_type=F32,
+            )
+            term = one if term is None else term + one
+        ends = [jnp.zeros((n * slab, w_ref.shape[1]), F32) for n in (2 - e, e)]
+        parts = [v for v in (ends[0], term, ends[1]) if v.shape[0] > 0]
+        padded = jnp.concatenate(parts, axis=0)
+        total = padded if total is None else total + padded
+    return total
+
+
+def edge_dots(cols_ref, w_ref, rows, slab, reverse):
+    terms = []
+    span = w_ref.shape[1] * 3
+    for e in range(3):
+        a = 2 - e if reverse else e
+        term = None
+        for t in range(3):
+            at = slice(t * span, (t + 1) * span)
+            if e == 0:
+                left = cols_ref[0 : 2 * slab, at]
+            elif e == 1:
+                left = jnp.concatenate(
+                    [cols_ref[slab : 2 * slab, at], cols_ref[(rows + 2) * slab : (rows + 3) * slab, at]], axis=0
+                )
+            else:
+                left = cols_ref[(rows + 2) * slab : (rows + 4) * slab, at]
+            one = jnp.dot(
+                left, w_ref[(t * 3 + a) * span : (t * 3 + a + 1) * span, :], preferred_element_type=F32
+            )
+            term = one if term is None else term + one
+        terms.append(term)
+    return jnp.concatenate(
+        [
+            terms[0][:slab] + terms[1][:slab],
+            terms[0][slab:],
+            jnp.zeros(((rows - 2) * slab, w_ref.shape[1]), F32),
+            terms[2][:slab],
+            terms[2][slab:] + terms[1][slab:],
+        ],
+        axis=0,
+    )
+
+
 def kernel(
     cfg,
     seg, x_hbm, w1_hbm, w2_hbm, c_hbm,
     pooled, in_grad, out1, out2,
     x_in, w1, w2, c_in, g_tmp, in_sem, x_halo, g_halo, cols_x, cols_h, cols_g, cols_a, w1t, w2t, pool_tmp,
-    seg_rows, mask_rows, x_out, x_got, hid_out, hid_got, cot_got, act_got, g_got, turned, flat,
+    own_x, own_g, mask_rows, c_flat, early_out, early_got, late_out, late_got, act_got, g_got, turned, flat,
     recv_a, sum_a, send_c, recv_c, every, spread,
-    h_send, h_recv, x_send, x_recv, s_send, s_recv, k_send, k_recv, g_send, g_recv, t_send, t_recv,
+    h_send, h_recv, x_send, x_recv, g_send, g_recv, t_send, t_recv,
     a_send, a_recv, c_send, c_recv, d_send, d_recv,
 ):
     n_tile, n_dp, share, quarter, part, unit, n_unit, scale = cfg
@@ -87,6 +141,10 @@
     lanes = wide * slab
     per_tap, per_quarter = ch // unit, quarter // unit
     slot = part // per_quarter
+    own_lanes = cells // ch
+    cot_at = own_lanes * part
+    seg_at = cot_at + cells // 4
+    edge_at = (own_lanes + 1) * part
     margin = (spread.shape[1] - share) // 2
     block = n_unit * slot
 
@@ -129,14 +187,15 @@
             dst[tap * ch : (tap + 1) * ch, :] = src[tap * ch : (tap + 1) * ch, :].T
 
     if part > quarter:
-        x_out[:, quarter:, :] = jnp.zeros((n_dp, part - quarter, lanes), BF16)
-        hid_out[:, quarter:, :] = jnp.zeros((n_dp, part - quarter, lanes), BF16)
+        early_out[...] = jnp.zeros(early_out.shape, BF16)
+        late_out[...] = jnp.zeros(late_out.shape, BF16)
     lane = lax.broadcasted_iota(jnp.int32, (16, 2 * slab), 1)
     frame = lax.rem(lax.div(lane, cols), frames)
     number = jnp.zeros((16, 2 * slab), F32)
     for f in range(frames):
         number = jnp.where(frame == f, seg[0, f].astype(F32), number)
-    seg_rows[dp] = number.astype(BF16)
+    for q in range(n_dp):
+        early_out[q, seg_at : seg_at + 16, :] = number.astype(BF16)
 
     @pl.when(tile == 0)
     def _():
@@ -154,6 +213,7 @@
     pl.semaphore_wait(barrier, n_dp - 1 + n_z - 1 + beside)
 
     g_rows = c_in.shape[0]
+    c_flat[...] = c_in[...].astype(F32).reshape(cells // 4, ch).astype(BF16)
 
     def halo(side):
         peer = {"tile": tile - 1 if side == 0 else tile + 1}
@@ -165,7 +225,9 @@
                 device_id=peer, device_id_type=MESH,
             ),
             pltpu.make_async_remote_copy(
-                src_ref=c_in.at[0:1] if side == 0 else c_in.at[g_rows - 1 : g_rows],
+                src_ref=c_flat.at[0 : slab // 2]
+                if side == 0
+                else c_flat.at[(g_rows - 1) * slab // 2 : g_rows * slab // 2],
                 dst_ref=g_halo.at[1 - side],
                 send_sem=h_send.at[2 + side], recv_sem=h_recv.at[2 + 1 - side],
                 device_id=peer, device_id_type=MESH,
@@ -200,29 +262,26 @@
         for copy in copies:
             copy.wait()
 
-    copies_cot = to_dp(lambda q: c_in, cot_got.at[dp], k_send, k_recv)
-    copies_seg = to_dp(lambda q: seg_rows.at[dp], seg_rows.at[dp], s_send, s_recv)
-    start(copies_cot)
-    start(copies_seg)
-    cot_got[dp] = c_in[...]
-
-    def deal(v, out, at):
+    def deal(v, out, base):
         v = v.reshape(-1, ch).T.astype(BF16)
-        for q in range(n_dp):
-            out[q, 0:quarter, at : at + v.shape[1]] = v[q * quarter : (q + 1) * quarter]
+        for p in range(v.shape[1] // ch):
+            for q in range(n_dp):
+                at = base + p * part
+                out[q, at : at + quarter, :] = v[q * quarter : (q + 1) * quarter, p * ch : (p + 1) * ch]
+
+    def dealt(got, d, base, n):
+        return [got[d, base + p * part : base + (p + 1) * part, :].astype(F32) for p in range(n)]
 
     mine = x_in[...].astype(F32)
-    deal(mine, x_out, 0)
-    copies_x = [
-        to_dp(lambda q: x_out.at[q, :, 0:cells], x_got.at[dp, :, 0:cells], x_send.at[0], x_recv.at[0]),
-        to_dp(lambda q: x_out.at[q, :, cells:], x_got.at[dp, :, cells:], x_send.at[1], x_recv.at[1]),
-    ]
-    start(copies_x[0])
-
-    load_w1.wait()
+    for q in range(n_dp):
+        early_out[q, cot_at:seg_at, :] = c_flat[...]
+    deal(mine, early_out, 0)
+    copies_early = to_dp(lambda q: early_out.at[q], early_got.at[dp], x_send, x_recv)
+    start(copies_early)
+    early_got[dp] = early_out[dp]
+
     load_w2.wait()
     flip(w2, w2t)
-    flip(w1, w1t)
     same = [None]
     for t in range(1, 3):
         same.append(
@@ -230,6 +289,24 @@
             + [jnp.where(seg[0, f] == seg[0, f - t], 1.0, 0.0).astype(F32) for f in range(t, frames)]
         )
 
+    def four(v):
+        return v.reshape(v.shape[0], frames, cols, ch)
+
+    def grow(v):
+        n = v.shape[0] * 2 // slab
+        v = v.astype(F32) * 0.25
+        g_tmp[pl.ds(0, n * slab // 2, stride=2), :] = v
+        g_tmp[pl.ds(1, n * slab // 2, stride=2), :] = v
+        v = g_tmp[0 : n * slab, :].reshape(n, slab, ch)
+        return jnp.stack([v, v], axis=1).reshape(2 * n, slab, ch)
+
+    g_mine = grow(c_flat[...])
+    fill_columns(cols_g, four(g_mine), same, True, 2)
+    own_g[...] = own_dots(cols_g, w2t, rows, slab, True)
+    fill_columns(cols_x, mine, same, False, 2)
+    load_w1.wait()
+    own_x[...] = own_dots(cols_x, w1, rows, slab, False)
+
     @pl.when(tile > 0)
     def _():
         for copy in halo(0):
@@ -244,27 +321,16 @@
         for copy in halo(0):
             copy.wait_recv()
 
-    def four(v):
-        return v.reshape(v.shape[0], frames, cols, ch)
-
-    x_all = jnp.concatenate([x_halo[0].astype(F32), mine, x_halo[1].astype(F32)], axis=0)
-    copies_hid = to_dp(lambda q: hid_out.at[q], hid_got.at[dp], t_send, t_recv)
+    x_low = x_halo[0].astype(F32)
+    x_high = x_halo[1].astype(F32)
+    deal(jnp.concatenate([x_high[:1], x_low[1:]], axis=0), late_out, edge_at)
+    fill_columns(cols_x, x_low, same, False, 0)
+    fill_columns(cols_x, x_high, same, False, rows + 2)
+    first = own_x[...] + edge_dots(cols_x, w1, rows, slab, False)
+    sigma = 1.0 / (1.0 + jnp.exp(-first))
+    copies_hid = to_dp(lambda q: late_out.at[q], late_got.at[dp], t_send, t_recv)
     copies_act = to_dp(lambda q: act_got.at[dp], act_got.at[dp], g_send, g_recv)
 
-    deal(jnp.concatenate([x_all[wide : wide + 1], x_all[1:2]], axis=0), x_out, cells)
-    start(copies_x[1])
-    x_got[dp] = x_out[dp]
-    fill_columns(cols_x, x_all, same, False)
-    c_all = jnp.concatenate([g_halo[0], c_in[...], g_halo[1]], axis=0).astype(F32) * 0.25
-    half = (g_rows + 2) * slab // 2
-    c_all = c_all.reshape(half, ch)
-    g_tmp[pl.ds(0, half, stride=2), :] = c_all
-    g_tmp[pl.ds(1, half, stride=2), :] = c_all
-    g_all = g_tmp[...].reshape(g_rows + 2, slab, ch)
-    g_all = jnp.stack([g_all, g_all], axis=1).reshape(2 * g_all.shape[0], slab, ch)
-
-    first = conv_dots(cols_x, w1, 0, wide, slab, False)
-    sigma = 1.0 / (1.0 + jnp.exp(-first))
     top = jnp.where(tile > 0, 1.0, 0.0).astype(F32)
     low = jnp.where(tile < n_tile - 1, 1.0, 0.0).astype(F32)
 
@@ -283,11 +349,11 @@
     def copies_a(g):
         return [
             pltpu.make_async_remote_copy(
-                src_ref=flat.at[g, window(2 * k + 1 - core)], dst_ref=recv_a.at[g, k],
-                send_sem=a_send.at[g, k], recv_sem=a_recv.at[g, k],
+                src_ref=flat.at[g, window(2 * lax.rem(z + j, n_z) + 1 - core)], dst_ref=recv_a.at[g, j],
+                send_sem=a_send.at[g, j], recv_sem=a_recv.at[g, j],
                 device_id={"tile": tile + 1 - 2 * core}, device_id_type=MESH,
             )
-            for k in range(n_z)
+            for j in range(n_z)
         ]
 
     def copies_c(g):
@@ -307,7 +373,7 @@
         return lax.rem(dp + n_dp - i, n_dp)
 
     def make_masks(d):
-        number = seg_rows[d].astype(F32)[0:8]
+        number = early_got[d, seg_at : seg_at + 16, :].astype(F32)[0:8]
         at = lax.broadcasted_iota(jnp.int32, (8, 2 * slab), 1)
         when = lax.rem(lax.div(at, cols), frames)
         col = lax.rem(at, cols)
@@ -320,8 +386,7 @@
                 inside = jnp.where((col + (b - 1) >= 0) & (col + (b - 1) < cols), keep, 0.0)
                 mask_rows[d, t * 3 + b] = inside
 
-    def turn(g, d, got):
-        v = got[d].astype(F32)[0:part]
+    def turn(g, d, v):
         for t in range(3):
             for b in range(3):
                 shift = t * cols - (b - 1)
@@ -338,17 +403,25 @@
         term = jnp.dot(turned[g, d], right, preferred_element_type=F32)
         flat[g] = term if fresh else flat[g] + term
 
+    def step_a(g):
+        copies = copies_a(g)
+        for j in (*range(1, n_z), 0):
+            copies[j].start()
+
     def step_b(g):
-        wait(copies_a(g))
-        for k in range(n_z):
-            sum_a[g, k] = flat[g, window(2 * k + core), :] + recv_a[g, k]
-        for j in range(1, n_z):
-            send_c[g, j - 1] = sum_a[g, lax.rem(z + j, n_z)].astype(BF16)
-        start(copies_c(g))
+        pairs, sends = copies_a(g), copies_c(g)
+        for j in (*range(1, n_z), 0):
+            pairs[j].wait()
+            total = flat[g, window(2 * lax.rem(z + j, n_z) + core), :] + recv_a[g, j]
+            if j > 0:
+                send_c[g, j - 1] = total.astype(BF16)
+                sends[j - 1].start()
+            else:
+                sum_a[g] = total
 
     def step_c(g):
         wait(copies_c(g))
-        total = sum_a[g, z]
+        total = sum_a[g]
         for j in range(1, n_z):
             total = total + recv_c[g, j - 1].astype(F32)
         every[g, dp] = (total * scale).astype(BF16)
@@ -367,43 +440,39 @@
 
     hidden = edges(first * sigma)
     by_row = hidden.reshape(wide, slab, ch)
-    deal(jnp.concatenate([by_row[1:], by_row[:1]], axis=0), hid_out, 0)
+    deal(jnp.concatenate([by_row[1:], by_row[:1]], axis=0), late_out, 0)
     start(copies_hid)
-    hid_got[dp] = hid_out[dp]
-    g_own = g_all[2 : 2 + rows].reshape(cells, ch)
-    fill_columns(cols_g, four(g_all), same, True)
-    hidden_grad = conv_dots(cols_g, w2t, 0, wide, slab, True)
+    late_got[dp] = late_out[dp]
+    g_own = g_mine.reshape(cells, ch)
+    fill_columns(cols_g, four(grow(g_halo[0])), same, True, 0)
+    fill_columns(cols_g, four(grow(g_halo[1])), same, True, rows + 2)
+    hidden_grad = own_g[...] + edge_dots(cols_g, w2t, rows, slab, True)
     act = edges(hidden_grad * sigma * (1.0 + first * (1.0 - sigma)))
     act_got[dp] = act[1 : 1 + rows].reshape(cells, ch).astype(BF16)
     start(copies_act)
-
-    wait(copies_seg)
+    flip(w1, w1t)
+
+    wait(copies_early)
     for d in range(n_dp):
         make_masks(d)
-    wait(copies_cot)
-    for d in range(n_dp):
-        v = (cot_got[d].astype(F32) * 0.25).reshape(cells // 4, ch)
-        g_tmp[pl.ds(0, cells // 4, stride=2), :] = v
-        g_tmp[pl.ds(1, cells // 4, stride=2), :] = v
-        v = g_tmp[0 : cells // 2, :].astype(BF16).reshape(rows // 2, slab, ch)
-        g_got[d] = jnp.stack([v, v], axis=1).reshape(cells, ch)
-    wait(copies_x[0])
-    wait(copies_x[1])
-    for d in range(n_dp):
-        turn(0, d, x_got)
+        g_got[d] = grow(early_got[d, cot_at:seg_at, :]).reshape(cells, ch).astype(BF16)
     fill_columns(cols_h, four(hidden), same, False)
     for i in range(n_dp):
         if i > 0:
             copies_hid[i - 1].wait()
-        turn(1, sender(i), hid_got)
+        parts = dealt(late_got, sender(i), 0, own_lanes + 1)
+        turn(1, sender(i), jnp.concatenate(parts, axis=1))
         partial_sum(1, sender(i), g_got[sender(i)], i == 0)
-    start(copies_a(1))
+    step_a(1)
+    for d in range(n_dp):
+        parts = dealt(early_got, d, 0, own_lanes) + dealt(late_got, d, edge_at, 1)
+        turn(0, d, jnp.concatenate(parts, axis=1))
+    step_b(1)
     for i in range(n_dp):
         if i > 0:
             copies_act[i - 1].wait()
         partial_sum(0, sender(i), act_got[sender(i)], i == 0)
-    start(copies_a(0))
-    step_b(1)
+    step_a(0)
     step_b(0)
 
     second = conv_dots(cols_h, w2, 0, rows, slab, False)
@@ -485,7 +554,7 @@
             pltpu.VMEM(((rows // 2 + 2) * slab, ch), F32),
             sem((2 + rows + rows // 2,)),
             pltpu.VMEM((2, 2, frames, cols, ch), BF16),
-            pltpu.VMEM((2, 1, frames, cols // 2, ch), BF16),
+            pltpu.VMEM((2, frames * cols // 2, ch), BF16),
             pltpu.VMEM(((rows + 4) * slab, 9 * ch), BF16),
             pltpu.VMEM(((rows + 2) * slab, 9 * ch), BF16),
             pltpu.VMEM(((rows + 4) * slab, 9 * ch), BF16),
@@ -493,26 +562,25 @@
             pltpu.VMEM((taps, ch), BF16),
             pltpu.VMEM((taps, ch), BF16),
             pltpu.VMEM((cells // 2, ch), F32),
-            pltpu.VMEM((n_dp, 16, 2 * slab), BF16),
+            pltpu.VMEM((lanes, ch), F32),
+            pltpu.VMEM((lanes, ch), F32),
             pltpu.VMEM((n_dp, 9, 8, 2 * slab), F32),
-            pltpu.VMEM((n_dp, part, lanes), BF16),
-            pltpu.VMEM((n_dp, part, lanes), BF16),
-            pltpu.VMEM((n_dp, part, lanes), BF16),
-            pltpu.VMEM((n_dp, part, lanes), BF16),
-            pltpu.VMEM((n_dp, rows // 2, frames, cols // 2, ch), BF16),
+            pltpu.VMEM((cells // 4, ch), BF16),
+            pltpu.VMEM((n_dp, cells // ch * part + cells // 4 + 16, ch), BF16),
+            pltpu.VMEM((n_dp, cells // ch * part + cells // 4 + 16, ch), BF16),
+            pltpu.VMEM((n_dp, (cells // ch + 2) * part, ch), BF16),
+            pltpu.VMEM((n_dp, (cells // ch + 2) * part, ch), BF16),
             pltpu.VMEM((n_dp, cells, ch), BF16),
             pltpu.VMEM((n_dp, cells, ch), BF16),
             pltpu.VMEM((2, n_dp, taps // ch * part, cells), BF16),
             pltpu.VMEM((2, taps // ch * part, ch), F32),
             pltpu.VMEM((2, n_z, block, ch), F32),
-            pltpu.VMEM((2, n_z, block, ch), F32),
+            pltpu.VMEM((2, block, ch), F32),
             pltpu.VMEM((2, n_z - 1, block, ch), BF16),
             pltpu.VMEM((2, n_z - 1, block, ch), BF16),
             pltpu.VMEM((2, n_dp, block, ch), BF16),
             pltpu.VMEM((2, span, ch), F32),
             sem((4,)), sem((4,)),
-            sem((2, n_dp - 1)), sem((2, n_dp - 1)),
-            sem((n_dp - 1,)), sem((n_dp - 1,)),
             sem((n_dp - 1,)), sem((n_dp - 1,)),
             sem((n_dp - 1,)), sem((n_dp - 1,)),
             sem((n_dp - 1,)), sem((n_dp - 1,)),

time: 30.7 us -> 28.3 us (0.922)
  Pallas kernels: 29.9 us -> 27.5 us
    pallas_call x1, Pallas kernels: 29.1 us -> 26.7 us  [local(): pl.pallas_call(functools.partial(kernel, (n_tile, n_dp, share, quarter, p...]
where the time goes in v5:
time: 28.3 us; the launch traced here: 28.2 us
  Pallas kernels  27.5 us (97%)
  between operations  0.64 us (2%)
    pallas_call x1, Pallas kernels, local(): pl.pallas_call(functools.partial(kernel, (n_tile, n_dp, share, quarter, p...  26.7 us
    pallas_call x1, Pallas kernels, local(): pl.pallas_call(hand_out, out_shape=shapes, in_specs=[pl.BlockSpec(memory_...  0.84 us

profile of v5, /device:TPU:0, one launch (start us, length us, event | category | flops | bytes accessed | tf_op | source)
XLA Modules:
  0.0 28.2 jit_solution(3897996915710171747)
XLA Ops:
  0.6 26.7 %shard_map.84 = (f32[1,8,2,4,128]{4,3,2,1,0:T(4,128)S(1)}, f32[1,8,4,8,128]{4,3,2,1,0:T(8,128)S(1)}, f32[432,128]{1,0:T(8,128)S(1)}, f32[432,128]{1,0:T(8,128)S(1)}) custom-call(s32[1,8]{1,0:T(1,128)} %seg.1, bf16[1,8,4,8,128]{4,3,2,1,0:T(8,128)(2,1)} %x_hbm.1, bf16[3456,128]{1,0:T(8,128)(2,1)} %w1_hbm.1, bf16[3456,128]{1,0:T(8,128)(2,1)} %w2_hbm.1, ...), custom_call_target="tpu_custom_call" | custom-call | tf_op jit(solution)/shard_map/pallas_call | solution.py:544
  27.3 0.8 %shard_map.85 = (f32[1,8,2,4,128]{4,3,2,1,0:T(4,128)}, f32[1,8,4,8,128]{4,3,2,1,0:T(8,128)}, f32[432,128]{1,0:T(8,128)}, f32[432,128]{1,0:T(8,128)}) custom-call(f32[1,8,2,4,128]{4,3,2,1,0:T(4,128)S(1)} %get-tuple-element.8.refs_0_, f32[1,8,4,8,128]{4,3,2,1,0:T(8,128)S(1)} %get-tuple-element.9.refs_1_, f32[432,128]{1,0:T(8,128)S(1)} %get-tuple-element.10.refs_2_, ...), custom_call_target="tpu_custom_call" | custom-call | tf_op jit(solution)/shard_map/pallas_call | solution.py:596

commit v6 on v5

--- a/solution.py
+++ b/solution.py
@@ -120,10 +120,10 @@
     cfg,
     seg, x_hbm, w1_hbm, w2_hbm, c_hbm,
     pooled, in_grad, out1, out2,
-    x_in, w1, w2, c_in, g_tmp, in_sem, x_halo, g_halo, cols_x, cols_h, cols_g, cols_a, w1t, w2t, pool_tmp,
-    own_x, own_g, mask_rows, c_flat, early_out, early_got, late_out, late_got, act_got, g_got, turned, flat,
+    x_in, w1, w2, c_in, g_tmp, in_sem, edge_out, edge_in, cols_x, cols_h, cols_g, cols_a, w1t, w2t, pool_tmp,
+    own_x, own_g, mid_got, mask_rows, c_flat, early_out, early_got, late_out, late_got, act_got, g_got, turned, flat,
     recv_a, sum_a, send_c, recv_c, every, spread,
-    h_send, h_recv, x_send, x_recv, g_send, g_recv, t_send, t_recv,
+    h_send, h_recv, m_send, m_recv, x_send, x_recv, g_send, g_recv, t_send, t_recv,
     a_send, a_recv, c_send, c_recv, d_send, d_recv,
 ):
     n_tile, n_dp, share, quarter, part, unit, n_unit, scale = cfg
@@ -199,69 +199,21 @@
 
     @pl.when(tile == 0)
     def _():
-        x_halo[0] = jnp.zeros(x_halo.shape[1:], BF16)
-        g_halo[0] = jnp.zeros(g_halo.shape[1:], BF16)
+        edge_in[0] = jnp.zeros(edge_in.shape[1:], BF16)
 
     @pl.when(tile == n_tile - 1)
     def _():
-        x_halo[1] = jnp.zeros(x_halo.shape[1:], BF16)
-        g_halo[1] = jnp.zeros(g_halo.shape[1:], BF16)
+        edge_in[1] = jnp.zeros(edge_in.shape[1:], BF16)
 
     for copy in load_x + load_c:
         copy.wait()
-    beside = jnp.where(tile > 0, 1, 0) + jnp.where(tile < n_tile - 1, 1, 0)
-    pl.semaphore_wait(barrier, n_dp - 1 + n_z - 1 + beside)
-
-    g_rows = c_in.shape[0]
     c_flat[...] = c_in[...].astype(F32).reshape(cells // 4, ch).astype(BF16)
-
-    def halo(side):
-        peer = {"tile": tile - 1 if side == 0 else tile + 1}
-        return (
-            pltpu.make_async_remote_copy(
-                src_ref=x_in.at[0:2] if side == 0 else x_in.at[rows - 2 : rows],
-                dst_ref=x_halo.at[1 - side],
-                send_sem=h_send.at[side], recv_sem=h_recv.at[1 - side],
-                device_id=peer, device_id_type=MESH,
-            ),
-            pltpu.make_async_remote_copy(
-                src_ref=c_flat.at[0 : slab // 2]
-                if side == 0
-                else c_flat.at[(g_rows - 1) * slab // 2 : g_rows * slab // 2],
-                dst_ref=g_halo.at[1 - side],
-                send_sem=h_send.at[2 + side], recv_sem=h_recv.at[2 + 1 - side],
-                device_id=peer, device_id_type=MESH,
-            ),
-        )
-
-    @pl.when(tile > 0)
-    def _():
-        for copy in halo(0):
-            copy.start()
-
-    @pl.when(tile < n_tile - 1)
-    def _():
-        for copy in halo(1):
-            copy.start()
-
-    def to_dp(src, dst, sends, recvs):
-        return [
-            pltpu.make_async_remote_copy(
-                src_ref=src(lax.rem(dp + i, n_dp)), dst_ref=dst,
-                send_sem=sends.at[i - 1], recv_sem=recvs.at[i - 1],
-                device_id={"dp": lax.rem(dp + i, n_dp)}, device_id_type=MESH,
-            )
-            for i in range(1, n_dp)
-        ]
-
-    def start(copies):
-        for copy in copies:
-            copy.start()
-
-    def wait(copies):
-        for copy in copies:
-            copy.wait()
-
+    mine = x_in[...].astype(F32)
+    flat_x = mine.reshape(cells, ch).astype(BF16)
+    edge_out[0, 0 : 2 * slab, :] = flat_x[: 2 * slab]
+    edge_out[1, 0 : 2 * slab, :] = flat_x[cells - 2 * slab :]
+    edge_out[0, 2 * slab :, :] = c_flat[0 : slab // 2, :]
+    edge_out[1, 2 * slab :, :] = c_flat[cells // 4 - slab // 2 :, :]
     def deal(v, out, base):
         v = v.reshape(-1, ch).T.astype(BF16)
         for p in range(v.shape[1] // ch):
@@ -269,19 +221,9 @@
                 at = base + p * part
                 out[q, at : at + quarter, :] = v[q * quarter : (q + 1) * quarter, p * ch : (p + 1) * ch]
 
-    def dealt(got, d, base, n):
-        return [got[d, base + p * part : base + (p + 1) * part, :].astype(F32) for p in range(n)]
-
-    mine = x_in[...].astype(F32)
     for q in range(n_dp):
         early_out[q, cot_at:seg_at, :] = c_flat[...]
     deal(mine, early_out, 0)
-    copies_early = to_dp(lambda q: early_out.at[q], early_got.at[dp], x_send, x_recv)
-    start(copies_early)
-    early_got[dp] = early_out[dp]
-
-    load_w2.wait()
-    flip(w2, w2t)
     same = [None]
     for t in range(1, 3):
         same.append(
@@ -302,10 +244,68 @@
 
     g_mine = grow(c_flat[...])
     fill_columns(cols_g, four(g_mine), same, True, 2)
+    fill_columns(cols_x, mine, same, False, 2)
+    beside = jnp.where(tile > 0, 1, 0) + jnp.where(tile < n_tile - 1, 1, 0)
+    pl.semaphore_wait(barrier, n_dp - 1 + n_z - 1 + beside)
+
+
+    def halo(side):
+        return [
+            pltpu.make_async_remote_copy(
+                src_ref=edge_out.at[side], dst_ref=edge_in.at[1 - side],
+                send_sem=h_send.at[side], recv_sem=h_recv.at[1 - side],
+                device_id={"tile": tile - 1 if side == 0 else tile + 1}, device_id_type=MESH,
+            )
+        ]
+
+    @pl.when(tile > 0)
+    def _():
+        for copy in halo(0):
+            copy.start()
+
+    @pl.when(tile < n_tile - 1)
+    def _():
+        for copy in halo(1):
+            copy.start()
+
+    def to_dp(src, dst, sends, recvs):
+        return [
+            pltpu.make_async_remote_copy(
+                src_ref=src(lax.rem(dp + i, n_dp)), dst_ref=dst,
+                send_sem=sends.at[i - 1], recv_sem=recvs.at[i - 1],
+                device_id={"dp": lax.rem(dp + i, n_dp)}, device_id_type=MESH,
+            )
+            for i in range(1, n_dp)
+        ]
+
+    def start(copies):
+        for copy in copies:
+            copy.start()
+
+    def wait(copies):
+        for copy in copies:
+            copy.wait()
+
+    def dealt(got, d, base, n):
+        return [got[d, base + p * part : base + (p + 1) * part, :].astype(F32) for p in range(n)]
+
+    copies_early = to_dp(lambda q: early_out.at[q], early_got.at[dp], x_send, x_recv)
+    start(copies_early)
+    early_got[dp] = early_out[dp]
+
+    load_w2.wait()
+    flip(w2, w2t)
     own_g[...] = own_dots(cols_g, w2t, rows, slab, True)
-    fill_columns(cols_x, mine, same, False, 2)
     load_w1.wait()
     own_x[...] = own_dots(cols_x, w1, rows, slab, False)
+    middle = slice(2 * slab, rows * slab)
+    inner = (rows - 2) * slab
+    mid = own_x[middle, :]
+    mid_sigma = 1.0 / (1.0 + jnp.exp(-mid))
+    mid_act = own_g[middle, :] * mid_sigma * (1.0 + mid * (1.0 - mid_sigma))
+    mid_got[dp] = mid_act.astype(BF16)
+    copies_mid = to_dp(lambda q: mid_got.at[dp], mid_got.at[dp], m_send, m_recv)
+    start(copies_mid)
 
     @pl.when(tile > 0)
     def _():
@@ -321,8 +321,7 @@
         for copy in halo(0):
             copy.wait_recv()
 
-    x_low = x_halo[0].astype(F32)
-    x_high = x_halo[1].astype(F32)
+    x_low, x_high = (edge_in[n, 0 : 2 * slab, :].astype(F32).reshape(2, frames, cols, ch) for n in range(2))
     deal(jnp.concatenate([x_high[:1], x_low[1:]], axis=0), late_out, edge_at)
     fill_columns(cols_x, x_low, same, False, 0)
     fill_columns(cols_x, x_high, same, False, rows + 2)
@@ -386,18 +385,32 @@
                 inside = jnp.where((col + (b - 1) >= 0) & (col + (b - 1) < cols), keep, 0.0)
                 mask_rows[d, t * 3 + b] = inside
 
-    def turn(g, d, v):
+    def put(g, d, piece, uses):
         for t in range(3):
             for b in range(3):
                 shift = t * cols - (b - 1)
-                moved = v if shift == 0 else pltpu.roll(v, shift % lanes, 1)
+                moved = piece if shift == 0 else pltpu.roll(piece, shift % (2 * slab), 1)
                 if t > 0 or b != 1:
-                    keep = jnp.concatenate([mask_rows[d, t * 3 + b]] * (wide // 2), axis=1)
+                    keep = mask_rows[d, t * 3 + b]
                     moved = moved * jnp.concatenate([keep] * (part // 8), axis=0)
-                for a in range(3):
-                    w = moved if a == 1 else pltpu.roll(moved, (1 - a) * slab % lanes, 1)
+                moved = moved.astype(BF16)
+                for a, k in uses:
                     at = ((t * 3 + a) * 3 + b) * part
-                    turned[g, d, at : at + part, :] = w[:, 0:cells].astype(BF16)
+                    turned[g, d, at : at + part, k * ch : (k + 1) * ch] = moved
+
+    def between(before, after):
+        lower = lax.broadcasted_iota(jnp.int32, before.shape, 1) < slab
+        return jnp.where(lower, pltpu.roll(before, slab, 1), pltpu.roll(after, slab, 1))
+
+    def turn_own(g, d, own):
+        for k, piece in enumerate(own):
+            put(g, d, piece, [(1, k)])
+            if k > 0:
+                put(g, d, between(own[k - 1], piece), [(0, k), (2, k - 1)])
+
+    def turn_ends(g, d, own, ends):
+        put(g, d, between(ends, own[0]), [(0, 0)])
+        put(g, d, between(own[-1], ends), [(2, len(own) - 1)])
 
     def partial_sum(g, d, right, fresh):
         term = jnp.dot(turned[g, d], right, preferred_element_type=F32)
@@ -444,11 +457,11 @@
     start(copies_hid)
     late_got[dp] = late_out[dp]
     g_own = g_mine.reshape(cells, ch)
-    fill_columns(cols_g, four(grow(g_halo[0])), same, True, 0)
-    fill_columns(cols_g, four(grow(g_halo[1])), same, True, rows + 2)
+    fill_columns(cols_g, four(grow(edge_in[0, 2 * slab :, :])), same, True, 0)
+    fill_columns(cols_g, four(grow(edge_in[1, 2 * slab :, :])), same, True, rows + 2)
     hidden_grad = own_g[...] + edge_dots(cols_g, w2t, rows, slab, True)
     act = edges(hidden_grad * sigma * (1.0 + first * (1.0 - sigma)))
-    act_got[dp] = act[1 : 1 + rows].reshape(cells, ch).astype(BF16)
+    act_got[dp] = jnp.concatenate([act[1], act[rows]], axis=0).astype(BF16)
     start(copies_act)
     flip(w1, w1t)
 
@@ -456,22 +469,26 @@
     for d in range(n_dp):
         make_masks(d)
         g_got[d] = grow(early_got[d, cot_at:seg_at, :]).reshape(cells, ch).astype(BF16)
+        turn_own(0, d, dealt(early_got, d, 0, own_lanes))
     fill_columns(cols_h, four(hidden), same, False)
     for i in range(n_dp):
         if i > 0:
             copies_hid[i - 1].wait()
-        parts = dealt(late_got, sender(i), 0, own_lanes + 1)
-        turn(1, sender(i), jnp.concatenate(parts, axis=1))
+        *own, ends = dealt(late_got, sender(i), 0, own_lanes + 1)
+        turn_own(1, sender(i), own)
+        turn_ends(1, sender(i), own, ends)
         partial_sum(1, sender(i), g_got[sender(i)], i == 0)
     step_a(1)
     for d in range(n_dp):
-        parts = dealt(early_got, d, 0, own_lanes) + dealt(late_got, d, edge_at, 1)
-        turn(0, d, jnp.concatenate(parts, axis=1))
+        turn_ends(0, d, dealt(early_got, d, 0, own_lanes), dealt(late_got, d, edge_at, 1)[0])
     step_b(1)
     for i in range(n_dp):
+        d = sender(i)
         if i > 0:
+            copies_mid[i - 1].wait()
             copies_act[i - 1].wait()
-        partial_sum(0, sender(i), act_got[sender(i)], i == 0)
+        ends = act_got[d]
+        partial_sum(0, d, jnp.concatenate([ends[:slab], mid_got[d], ends[slab:]], axis=0), i == 0)
     step_a(0)
     step_b(0)
 
@@ -553,8 +570,8 @@
             pltpu.VMEM((rows // 2, frames, cols // 2, ch), BF16),
             pltpu.VMEM(((rows // 2 + 2) * slab, ch), F32),
             sem((2 + rows + rows // 2,)),
-            pltpu.VMEM((2, 2, frames, cols, ch), BF16),
-            pltpu.VMEM((2, frames * cols // 2, ch), BF16),
+            pltpu.VMEM((2, 2 * slab + slab // 2, ch), BF16),
+            pltpu.VMEM((2, 2 * slab + slab // 2, ch), BF16),
             pltpu.VMEM(((rows + 4) * slab, 9 * ch), BF16),
             pltpu.VMEM(((rows + 2) * slab, 9 * ch), BF16),
             pltpu.VMEM(((rows + 4) * slab, 9 * ch), BF16),
@@ -564,13 +581,14 @@
             pltpu.VMEM((cells // 2, ch), F32),
             pltpu.VMEM((lanes, ch), F32),
             pltpu.VMEM((lanes, ch), F32),
+            pltpu.VMEM((n_dp, cells - 2 * slab, ch), BF16),
             pltpu.VMEM((n_dp, 9, 8, 2 * slab), F32),
             pltpu.VMEM((cells // 4, ch), BF16),
             pltpu.VMEM((n_dp, cells // ch * part + cells // 4 + 16, ch), BF16),
             pltpu.VMEM((n_dp, cells // ch * part + cells // 4 + 16, ch), BF16),
             pltpu.VMEM((n_dp, (cells // ch + 2) * part, ch), BF16),
             pltpu.VMEM((n_dp, (cells // ch + 2) * part, ch), BF16),
-            pltpu.VMEM((n_dp, cells, ch), BF16),
+            pltpu.VMEM((n_dp, 2 * slab, ch), BF16),
             pltpu.VMEM((n_dp, cells, ch), BF16),
             pltpu.VMEM((2, n_dp, taps // ch * part, cells), BF16),
             pltpu.VMEM((2, taps // ch * part, ch), F32),
@@ -580,7 +598,8 @@
             pltpu.VMEM((2, n_z - 1, block, ch), BF16),
             pltpu.VMEM((2, n_dp, block, ch), BF16),
             pltpu.VMEM((2, span, ch), F32),
-            sem((4,)), sem((4,)),
+            sem((2,)), sem((2,)),
+            sem((n_dp - 1,)), sem((n_dp - 1,)),
             sem((n_dp - 1,)), sem((n_dp - 1,)),
             sem((n_dp - 1,)), sem((n_dp - 1,)),
             sem((n_dp - 1,)), sem((n_dp - 1,)),

time: 28.3 us -> 27.8 us (0.982)
  Pallas kernels: 27.5 us -> 27 us
    pallas_call x1, Pallas kernels: 26.7 us -> 26.2 us  [local(): pl.pallas_call(functools.partial(kernel, (n_tile, n_dp, share, quarter, p...]
where the time goes in v6:
time: 27.8 us; the launch traced here: 27.7 us
  Pallas kernels  27 us (97%)
  between operations  0.64 us (2%)
    pallas_call x1, Pallas kernels, local(): pl.pallas_call(functools.partial(kernel, (n_tile, n_dp, share, quarter, p...  26.2 us
    pallas_call x1, Pallas kernels, local(): pl.pallas_call(hand_out, out_shape=shapes, in_specs=[pl.BlockSpec(memory_...  0.84 us

profile of v6, /device:TPU:0, one launch (start us, length us, event | category | flops | bytes accessed | tf_op | source)
XLA Modules:
  0.0 27.7 jit_solution(830261040485780492)
XLA Ops:
  0.6 26.2 %shard_map.84 = (f32[1,8,2,4,128]{4,3,2,1,0:T(4,128)S(1)}, f32[1,8,4,8,128]{4,3,2,1,0:T(8,128)S(1)}, f32[432,128]{1,0:T(8,128)S(1)}, f32[432,128]{1,0:T(8,128)S(1)}) custom-call(s32[1,8]{1,0:T(1,128)} %seg.1, bf16[1,8,4,8,128]{4,3,2,1,0:T(8,128)(2,1)} %x_hbm.1, bf16[3456,128]{1,0:T(8,128)(2,1)} %w1_hbm.1, bf16[3456,128]{1,0:T(8,128)(2,1)} %w2_hbm.1, ...), custom_call_target="tpu_custom_call" | custom-call | tf_op jit(solution)/shard_map/pallas_call | solution.py:561
  26.8 0.8 %shard_map.85 = (f32[1,8,2,4,128]{4,3,2,1,0:T(4,128)}, f32[1,8,4,8,128]{4,3,2,1,0:T(8,128)}, f32[432,128]{1,0:T(8,128)}, f32[432,128]{1,0:T(8,128)}) custom-call(f32[1,8,2,4,128]{4,3,2,1,0:T(4,128)S(1)} %get-tuple-element.8.refs_0_, f32[1,8,4,8,128]{4,3,2,1,0:T(8,128)S(1)} %get-tuple-element.9.refs_1_, f32[432,128]{1,0:T(8,128)S(1)} %get-tuple-element.10.refs_2_, ...), custom_call_target="tpu_custom_call" | custom-call | tf_op jit(solution)/shard_map/pallas_call | solution.py:615
